TPU v7x, 32 devices: a whole 2x2x4 slice. The times are simulated.
32 devices in a mesh: section: 2 (over y), dp: 16 (over z, x, core).
Axes of the slice: x: 2, y: 2, z: 4, core: 2. Of those that a mesh axis runs over, the one named last changes fastest.
Arguments:
- patches: bfloat16 [12544, 768], P('dp'), may hold values from -6 to 6
- captions: bfloat16 [8192, 768], P('dp'), may hold values from -6 to 6
- segments: int32 [64, 128], P('dp'), may hold values from 0 to 3, never falling along the last dimension, each value on 1 to 64 neighbouring positions
- seg_images: int32 [64, 4], P('dp'), may hold values from 0 to 1
- attn_w: bfloat16 [2, 768, 4608], P('section'), may hold values from -0.9 to 0.9
- w_in: bfloat16 [2, 768, 3072], P('section'), may hold values from -0.21875 to 0.21875
- w_out: bfloat16 [2, 3072, 768], P('section'), may hold values from -0.109375 to 0.109375
- norm_gains: float32 [2, 3, 768], P('section'), may hold values from 0.5 to 1.5
- cotangent: bfloat16 [8192, 768], P('dp'), may hold values from -6 to 6
Outputs:
- decoded: bfloat16 [8192, 768], P('dp', 'section')
- caption_grad: float32 [8192, 768], P('dp', 'section')
- patch_grad: float32 [12544, 768], P('dp', 'section')
- attn_grad: float32 [2, 768, 4608], P('section', 'dp')
- w_in_grad: float32 [2, 768, 3072], P('section', 'dp')
- w_out_grad: float32 [2, 3072, 768], P('section', 'dp')
- gain_grad: float32 [2, 3, 768], P('section', None, 'dp')
Inputs may be any that keep to these rules, and one draw needn't show every extreme that they name: Every caption row has its 4 segments in order, numbered from 0. seg_images[r, s] names one of the 2 images of the group of caption row r.
All inputs are finite; a program needn't handle non-finite values.
Results may differ from a plain program's by a relative error of at most 0.015.
Values may be sent and summed in bfloat16 or wider, within the bound.
A program may use at most 320 MiB of HBM per device.

v0:
```python
import jax
import jax.numpy as jnp
from jax import lax
from jax.sharding import PartitionSpec as P

D = 768
FF = 3072
HEADS = 12
HEAD = 64
PATCHES = 196
ROW = 128
SEGS = 4
MICRO = 2
IMG_MB = 2
ROWS_MB = 2


NORM_EPS = 1e-06
SCORE_SCALE = 0.125
MASKED = -1e30
ROOT_HALF = 0.7071067811865476
INV_ROOT_TWO_PI = 0.3989422804014327


def shifted(block, axis, distance):
    devices = range(lax.axis_size(axis))
    route = [(i - distance, i) for i in devices if i - distance in devices]
    return lax.ppermute(block, axis, route)


def matmul(left_side, right_side):
    return jnp.dot(left_side, right_side, preferred_element_type=jnp.float32)


def matmul_nt(left_side, right_side):
    return lax.dot_general(
        left_side, right_side, (((1,), (1,)), ((), ())), preferred_element_type=jnp.float32
    )


def matmul_tn(left_side, right_side):
    return lax.dot_general(
        left_side, right_side, (((0,), (0,)), ((), ())), preferred_element_type=jnp.float32
    )


def norm_fwd(values, gain_row):
    row_mean = jnp.mean(values, -1, keepdims=True)
    centred = values - row_mean
    inverse = lax.rsqrt(jnp.mean(centred * centred, -1, keepdims=True) + NORM_EPS)
    normed = centred * inverse
    return ((normed * gain_row).astype(jnp.bfloat16), normed, inverse)


def norm_bwd(upstream, normed, inverse, gain_row):
    scaled = upstream * gain_row
    row_inner = (
        scaled
        - jnp.mean(scaled, -1, keepdims=True)
        - normed * jnp.mean(scaled * normed, -1, keepdims=True)
    )
    return (row_inner * inverse, jnp.sum(upstream * normed, 0))


def gelu_parts(hidden):
    normal_cdf = 0.5 * (1.0 + jax.scipy.special.erf(hidden * ROOT_HALF))
    return (
        hidden * normal_cdf,
        normal_cdf + hidden * INV_ROOT_TWO_PI * jnp.exp(-0.5 * hidden * hidden),
    )


def masked_scores(queries, key_rows, key_mask):
    scores = (
        jnp.einsum("bqhe,bkhe->bhqk", queries, key_rows, preferred_element_type=jnp.float32)
        * SCORE_SCALE
    )
    if key_mask is not None:
        scores = jnp.where(key_mask[:, None], scores, MASKED)
    return scores


def attend_fwd(queries, key_rows, values, key_mask):
    scores = masked_scores(queries, key_rows, key_mask)
    row_top = jnp.max(scores, -1, keepdims=True)
    log_total = jnp.log(jnp.sum(jnp.exp(scores - row_top), -1, keepdims=True)) + row_top
    attn_probs = jnp.exp(scores - log_total).astype(jnp.bfloat16)
    mixed = jnp.einsum("bhqk,bkhe->bqhe", attn_probs, values, preferred_element_type=jnp.float32)
    return (mixed.astype(jnp.bfloat16), log_total)


def attend_bwd(queries, key_rows, values, key_mask, log_total, grad_mixed):
    attn_probs = jnp.exp(masked_scores(queries, key_rows, key_mask) - log_total)
    grad_probs = jnp.einsum(
        "bqhe,bkhe->bhqk", grad_mixed, values, preferred_element_type=jnp.float32
    )
    row_inner = jnp.sum(grad_probs * attn_probs, -1, keepdims=True)
    grad_scores = (attn_probs * (grad_probs - row_inner)).astype(jnp.bfloat16)
    grad_query = (
        jnp.einsum("bhqk,bkhe->bqhe", grad_scores, key_rows, preferred_element_type=jnp.float32)
        * SCORE_SCALE
    )
    grad_key = (
        jnp.einsum("bhqk,bqhe->bkhe", grad_scores, queries, preferred_element_type=jnp.float32)
        * SCORE_SCALE
    )
    grad_value = jnp.einsum(
        "bhqk,bqhe->bkhe",
        attn_probs.astype(jnp.bfloat16),
        grad_mixed,
        preferred_element_type=jnp.float32,
    )
    return (grad_query, grad_key, grad_value)


def split_three(qkv_low, head_shape):
    return tuple(
        (qkv_low[:, index * D : (index + 1) * D].reshape(head_shape) for index in range(3))
    )


def attention_forward(resid, gain_row, attn_mat, head_shape, key_mask):
    a_low, a_hat, a_inv = norm_fwd(resid, gain_row)
    qkv_low = matmul(a_low, attn_mat[:, : 3 * D]).astype(jnp.bfloat16)
    queries, key_rows, values = split_three(qkv_low, head_shape)
    mixed, log_total = attend_fwd(queries, key_rows, values, key_mask)
    mixed_low = mixed.reshape(-1, D)
    return (
        resid + matmul(mixed_low, attn_mat[:, 3 * D : 4 * D]),
        (a_low, a_hat, a_inv, qkv_low, mixed_low, log_total),
    )


def attention_backward(
    upstream,
    a_low,
    a_hat,
    a_inv,
    qkv_low,
    mixed_low,
    log_total,
    key_mask,
    head_shape,
    attn_mat,
    gain_row,
):
    grad_att = upstream.astype(jnp.bfloat16)
    grad_mixed = (
        matmul_nt(grad_att, attn_mat[:, 3 * D : 4 * D]).astype(jnp.bfloat16).reshape(head_shape)
    )
    queries, key_rows, values = split_three(qkv_low, head_shape)
    grad_query, grad_key, grad_value = attend_bwd(
        queries, key_rows, values, key_mask, log_total, grad_mixed
    )
    grad_qkv = jnp.concatenate(
        [grad_query.reshape(-1, D), grad_key.reshape(-1, D), grad_value.reshape(-1, D)], 1
    ).astype(jnp.bfloat16)
    grad_input, grad_gain = norm_bwd(
        matmul_nt(grad_qkv, attn_mat[:, : 3 * D]), a_hat, a_inv, gain_row
    )
    return (upstream + grad_input, grad_gain, (a_low, grad_qkv, mixed_low, grad_att))


def mlp_forward(resid, gain_row, inner_w, outer_w):
    b_low, b_hat, b_inv = norm_fwd(resid, gain_row)
    activated, gelu_slope = gelu_parts(matmul(b_low, inner_w))
    act_low = activated.astype(jnp.bfloat16)
    return (resid + matmul(act_low, outer_w), (b_low, b_hat, b_inv, gelu_slope, act_low))


def mlp_backward(upstream, mlp_kept, inner_w, outer_w, gain_row):
    b_low, b_hat, b_inv, gelu_slope, act_low = mlp_kept
    grad_y = upstream.astype(jnp.bfloat16)
    grad_hidden = (matmul_nt(grad_y, outer_w) * gelu_slope).astype(jnp.bfloat16)
    grad_input, grad_gain = norm_bwd(matmul_nt(grad_hidden, inner_w), b_hat, b_inv, gain_row)
    return (upstream + grad_input, grad_gain, (b_low, grad_hidden, act_low, grad_y))


def encoder_forward(patch_rows, attn_mat, inner_w, outer_w, gain_set):
    head_shape = (IMG_MB, PATCHES, HEADS, HEAD)
    after_attn, attn_kept = attention_forward(
        patch_rows.astype(jnp.float32), gain_set[0], attn_mat, head_shape, None
    )
    after_mlp, mlp_kept = mlp_forward(after_attn, gain_set[1], inner_w, outer_w)
    c_low, c_hat, c_inv = norm_fwd(after_mlp, gain_set[2])
    context = matmul(c_low, attn_mat[:, 4 * D :]).astype(jnp.bfloat16)
    return (context, (attn_kept, mlp_kept, (c_low, c_hat, c_inv)))


def encoder_backward(patch_rows, grad_context, attn_mat, inner_w, outer_w, gain_set):
    head_shape = (IMG_MB, PATCHES, HEADS, HEAD)
    attn_kept, mlp_kept, norm_kept = encoder_forward(
        patch_rows, attn_mat, inner_w, outer_w, gain_set
    )[1]
    c_low, c_hat, c_inv = norm_kept
    grad_top, gain_top = norm_bwd(
        matmul_nt(grad_context, attn_mat[:, 4 * D :]), c_hat, c_inv, gain_set[2]
    )
    grad_mid, gain_mid, mlp_pairs = mlp_backward(grad_top, mlp_kept, inner_w, outer_w, gain_set[1])
    grad_input, gain_low, attn_pairs = attention_backward(
        grad_mid, *attn_kept, None, head_shape, attn_mat, gain_set[0]
    )
    gains = jnp.stack([gain_low, gain_mid, gain_top])
    return (grad_input, attn_pairs + mlp_pairs + (c_low, grad_context, gains))


def decoder_step(
    caption_rows, context, seg_rows, image_rows, cot_rows, attn_mat, inner_w, outer_w, gain_set
):
    head_shape = (ROWS_MB, ROW, HEADS, HEAD)
    cross_shape = (1, ROWS_MB * ROW, HEADS, HEAD)
    image_shape = (1, IMG_MB * PATCHES, HEADS, HEAD)
    position = jnp.arange(ROW)
    self_mask = (position[:, None] >= position[None, :])[None] & (
        seg_rows[:, :, None] == seg_rows[:, None, :]
    )
    seg_match = seg_rows[:, :, None] == jnp.arange(SEGS)[None, None, :]
    token_image = jnp.sum(jnp.where(seg_match, image_rows[:, None, :], 0), -1).reshape(1, -1)
    cross_mask = token_image[:, :, None] == (jnp.arange(IMG_MB * PATCHES) // PATCHES)[None, None, :]
    after_attn, attn_kept = attention_forward(
        caption_rows.astype(jnp.float32), gain_set[0], attn_mat, head_shape, self_mask
    )
    c_low, c_hat, c_inv = norm_fwd(after_attn, gain_set[1])
    cross_q = matmul(c_low, attn_mat[:, 4 * D : 5 * D]).astype(jnp.bfloat16).reshape(cross_shape)
    image_keys = context[:, :D].reshape(image_shape)
    image_values = context[:, D:].reshape(image_shape)
    crossed, cross_total = attend_fwd(cross_q, image_keys, image_values, cross_mask)
    crossed_low = crossed.reshape(-1, D)
    after_cross = after_attn + matmul(crossed_low, attn_mat[:, 5 * D :])
    after_mlp, mlp_kept = mlp_forward(after_cross, gain_set[2], inner_w, outer_w)
    grad_cross, gain_top, mlp_pairs = mlp_backward(
        cot_rows.astype(jnp.float32), mlp_kept, inner_w, outer_w, gain_set[2]
    )
    grad_cross_low = grad_cross.astype(jnp.bfloat16)
    grad_crossed = (
        matmul_nt(grad_cross_low, attn_mat[:, 5 * D :]).astype(jnp.bfloat16).reshape(cross_shape)
    )
    grad_query, grad_key, grad_value = attend_bwd(
        cross_q, image_keys, image_values, cross_mask, cross_total, grad_crossed
    )
    grad_cross_q = grad_query.reshape(-1, D).astype(jnp.bfloat16)
    grad_context = jnp.concatenate([grad_key.reshape(-1, D), grad_value.reshape(-1, D)], 1).astype(
        jnp.bfloat16
    )
    grad_norm, gain_mid = norm_bwd(
        matmul_nt(grad_cross_q, attn_mat[:, 4 * D : 5 * D]), c_hat, c_inv, gain_set[1]
    )
    grad_input, gain_low, attn_pairs = attention_backward(
        grad_cross + grad_norm, *attn_kept, self_mask, head_shape, attn_mat, gain_set[0]
    )
    gains = jnp.stack([gain_low, gain_mid, gain_top])
    cross_pairs = (c_low, grad_cross_q, crossed_low, grad_cross_low)
    return (after_mlp, grad_input, grad_context, attn_pairs + cross_pairs + mlp_pairs + (gains,))


def join_rows(kept_list, index):
    return jnp.concatenate([member[index] for member in kept_list], 0)


def encoder_weights(kept_list):
    parts = [join_rows(kept_list, index) for index in range(10)]
    gains = kept_list[0][10]
    for member in kept_list[1:]:
        gains = gains + member[10]
    return (
        matmul_tn(parts[0], parts[1]),
        matmul_tn(parts[2], parts[3]),
        matmul_tn(parts[8], parts[9]),
        matmul_tn(parts[4], parts[5]),
        matmul_tn(parts[6], parts[7]),
        gains,
    )


def decoder_weights(kept_list):
    parts = [join_rows(kept_list, index) for index in range(12)]
    gains = kept_list[0][12]
    for member in kept_list[1:]:
        gains = gains + member[12]
    last_cols = jnp.concatenate([matmul_tn(parts[4], parts[5]), matmul_tn(parts[6], parts[7])], 1)
    return (
        matmul_tn(parts[0], parts[1]),
        matmul_tn(parts[2], parts[3]),
        last_cols,
        matmul_tn(parts[8], parts[9]),
        matmul_tn(parts[10], parts[11]),
        gains,
    )


def weight_pass(is_first, enc_list, dec_list):
    return lax.cond(
        is_first,
        lambda operands: encoder_weights(operands[0]),
        lambda operands: decoder_weights(operands[1]),
        (enc_list, dec_list),
    )


def zero_set(shape_list):
    return tuple((jnp.zeros(shape, kind) for shape, kind in shape_list))


def pass_up(context):
    return shifted(context, "section", 1)


def pass_down(grad_context):
    return shifted(grad_context, "section", -1)


def local(patches, captions, segments, seg_images, attn_w, w_in, w_out, norm_gains, cotangent):
    attn_mat = attn_w[0]
    inner_w = w_in[0]
    outer_w = w_out[0]
    gain_set = norm_gains[0]
    is_first = lax.axis_index("section") == 0
    patch_block = IMG_MB * PATCHES
    caption_block = ROWS_MB * ROW
    low_kind = jnp.bfloat16
    wide_kind = jnp.float32
    enc_shapes = [
        ((patch_block, D), low_kind),
        ((patch_block, 3 * D), low_kind),
        ((patch_block, D), low_kind),
        ((patch_block, D), low_kind),
        ((patch_block, D), low_kind),
        ((patch_block, FF), low_kind),
        ((patch_block, FF), low_kind),
        ((patch_block, D), low_kind),
        ((patch_block, D), low_kind),
        ((patch_block, 2 * D), low_kind),
        ((3, D), wide_kind),
    ]
    dec_shapes = [
        ((caption_block, D), low_kind),
        ((caption_block, 3 * D), low_kind),
        ((caption_block, D), low_kind),
        ((caption_block, D), low_kind),
        ((caption_block, D), low_kind),
        ((caption_block, D), low_kind),
        ((caption_block, D), low_kind),
        ((caption_block, D), low_kind),
        ((caption_block, D), low_kind),
        ((caption_block, FF), low_kind),
        ((caption_block, FF), low_kind),
        ((caption_block, D), low_kind),
        ((3, D), wide_kind),
    ]
    empty_ctx = jnp.zeros((patch_block, 2 * D), jnp.bfloat16)
    empty_patch = jnp.zeros((patch_block, D), jnp.float32)
    empty_caption = jnp.zeros((caption_block, D), jnp.float32)
    context_in = empty_ctx
    grad_in = empty_ctx
    enc_list = []
    dec_list = []
    patch_rows_list = []
    decoded_list = []
    caption_rows_list = []
    for tick_index in range(MICRO + 2):
        enc_fwd = tick_index < MICRO
        enc_bwd = tick_index >= 2
        dec_on = 1 <= tick_index <= MICRO

        def encoder_tick(
            operands, tick_index=tick_index, enc_fwd=enc_fwd, enc_bwd=enc_bwd, dec_on=dec_on
        ):
            context_now, grad_now = operands
            send_up = empty_ctx
            if enc_fwd:
                start_row = tick_index * patch_block
                send_up = encoder_forward(
                    patches[start_row : start_row + patch_block],
                    attn_mat,
                    inner_w,
                    outer_w,
                    gain_set,
                )[0]
            results = [send_up, empty_ctx]
            if enc_bwd:
                start_row = (tick_index - 2) * patch_block
                grad_rows, enc_kept = encoder_backward(
                    patches[start_row : start_row + patch_block],
                    grad_now,
                    attn_mat,
                    inner_w,
                    outer_w,
                    gain_set,
                )
                results = results + [grad_rows, enc_kept]
            if dec_on:
                results = results + [empty_caption, empty_caption, zero_set(dec_shapes)]
            return tuple(results)

        def decoder_tick(
            operands, tick_index=tick_index, enc_fwd=enc_fwd, enc_bwd=enc_bwd, dec_on=dec_on
        ):
            context_now, grad_now = operands
            results = [empty_ctx]
            send_down = empty_ctx
            extra = []
            if dec_on:
                micro_index = tick_index - 1
                start_row = micro_index * caption_block
                start_seq = micro_index * ROWS_MB
                out_rows, grad_rows, send_down, dec_kept = decoder_step(
                    captions[start_row : start_row + caption_block],
                    context_now,
                    segments[start_seq : start_seq + ROWS_MB],
                    seg_images[start_seq : start_seq + ROWS_MB],
                    cotangent[start_row : start_row + caption_block],
                    attn_mat,
                    inner_w,
                    outer_w,
                    gain_set,
                )
                extra = [out_rows, grad_rows, dec_kept]
            results = results + [send_down]
            if enc_bwd:
                results = results + [empty_patch, zero_set(enc_shapes)]
            return tuple(results + extra)

        outcome = lax.cond(is_first, encoder_tick, decoder_tick, (context_in, grad_in))
        send_up, send_down = (outcome[0], outcome[1])
        rest = list(outcome[2:])
        if enc_bwd:
            patch_rows_list.append(rest[0])
            enc_list.append(rest[1])
            rest = rest[2:]
        if dec_on:
            decoded_list.append(rest[0])
            caption_rows_list.append(rest[1])
            dec_list.append(rest[2])
        if enc_fwd:
            context_in = pass_up(send_up)
        if dec_on:
            grad_in = pass_down(send_down)
    all_parts = weight_pass(is_first, enc_list, dec_list)
    shares = (
        lax.psum_scatter(all_parts[0], "dp", scatter_dimension=0, tiled=True),
        lax.psum_scatter(all_parts[1], "dp", scatter_dimension=0, tiled=True),
        lax.psum_scatter(all_parts[2], "dp", scatter_dimension=0, tiled=True),
        lax.psum_scatter(all_parts[3], "dp", scatter_dimension=0, tiled=True),
        lax.psum_scatter(all_parts[4], "dp", scatter_dimension=0, tiled=True),
        lax.psum_scatter(all_parts[5], "dp", scatter_dimension=1, tiled=True),
    )
    attn_share = jnp.concatenate([shares[0], shares[1], shares[2]], 1)
    patch_grad = jnp.concatenate(patch_rows_list, 0)
    decoded = jnp.concatenate(decoded_list, 0)
    caption_grad = jnp.concatenate(caption_rows_list, 0)
    half_width = D // 2
    sent_patch = shifted(patch_grad[:, half_width:].astype(jnp.bfloat16), "section", 1).astype(
        jnp.float32
    )
    patch_out = jnp.where(is_first, patch_grad[:, :half_width], sent_patch)
    got_decoded, got_grad = (
        shifted(decoded[:, :half_width].astype(jnp.bfloat16), "section", -1).astype(jnp.float32),
        shifted(caption_grad[:, :half_width].astype(jnp.bfloat16), "section", -1).astype(
            jnp.float32
        ),
    )
    decoded_out = jnp.where(is_first, got_decoded, decoded[:, half_width:]).astype(jnp.bfloat16)
    caption_out = jnp.where(is_first, got_grad, caption_grad[:, half_width:])
    return (
        decoded_out,
        caption_out,
        patch_out,
        attn_share[None],
        shares[3][None],
        shares[4][None],
        shares[5][None],
    )


def solution(mesh):
    placed = (
        P("dp", None),
        P("dp", None),
        P("dp", None),
        P("dp", None),
        P("section", None, None),
        P("section", None, None),
        P("section", None, None),
        P("section", None, None),
        P("dp", None),
    )
    return jax.shard_map(
        local,
        mesh=mesh,
        in_specs=placed,
        out_specs=(
            P("dp", "section"),
            P("dp", "section"),
            P("dp", "section"),
            P("section", "dp", None),
            P("section", "dp", None),
            P("section", "dp", None),
            P("section", None, "dp"),
        ),
        check_vma=False,
    )
```

profile of v0, /device:TPU:0, one launch (start us, length us, event | category | flops | bytes accessed | tf_op | source)
XLA Modules:
  0.0 1056.2 jit_solution(15088775600229996245)
XLA Ops:
  7.9 40.9 %conditional.5 = (bf16[392,1536]{1,0:T(8,128)(2,1)}) conditional(s32[]{:T(128)} %convert_element_type.352, () %tuple.49, (bf16[784,768]{1,0:T(8,128)(2,1)}, f32[3,768]{1,0:T(4,128)S(1)}, bf16[768,4608]{1,0:T(8,128)(2,1)}, bf16[768,3072]{1,0:T(8,128)(2,1)}, bf16[3072,768]{1,0:T(8,128)(2,1)}) %tuple.246), branch_computations={%region_0.0_spmd, %region_1.0_spmd} | conditional | flops 6734167552 | bytes 77639224 | solution.py:423
  10.7 3.9 convolution_convert_fusion
  18.0 3.0 reshape.875
  26.6 3.5 fusion.98
  35.6 8.7 fusion.357
  44.6 3.9 convolution_convert_fusion.1
  50.2 26.9 %collective-permute-done = bf16[392,1536]{1,0:T(8,128)(2,1)S(1)} collective-permute-done((bf16[392,1536]{1,0:T(8,128)(2,1)}, bf16[392,1536]{1,0:T(8,128)(2,1)S(1)}, u32[]{:S(2)}, u32[]{:S(2)}) %collective-permute-start) | collective-permute-done | bytes 1204256 | tf_op jit(solution)/shard_map/ppermute | solution.py:28
  77.1 53.2 %conditional.6 = (bf16[392,1536]{1,0:T(8,128)(2,1)}, bf16[392,1536]{0,1:T(8,128)(2,1)}, f32[256,768]{1,0:T(8,128)}, f32[256,768]{1,0:T(8,128)}, bf16[256,768]{1,...) conditional(s32[]{:T(128)} %convert_element_type.352, ...), branch_computations={%region_10.33_spmd, %region_33.42_spmd} | conditional | flops 9754902528 | bytes 296949408 | solution.py:423
  82.6 3.9 convolution_convert_fusion.10
  88.6 2.7 reshape.878
  95.4 3.5 fusion.193
  103.3 8.7 fusion.360
  112.3 3.9 convolution_convert_fusion.11
  130.4 57.6 %collective-permute-start.1 = (bf16[392,1536]{1,0:T(8,128)(2,1)}, bf16[392,1536]{1,0:T(8,128)(2,1)}, u32[]{:S(2)}, u32[]{:S(2)}) collective-permute-start(bf16[392,1536]{1,0:T(8,128)(2,1)} %get-tuple-element.346), channel_id=1, source_target_pairs={{0,16},{1,17},{2,18},{3,19},{4,20},{5,21},{6,22},{7,23},{8,24},{9,... | collective-permute-start | bytes 3612680 | tf_op jit(solution)/shard_map/ppermute | solution.py:28
  188.0 2.6 copy.456
  191.8 21.2 %collective-permute-done.1 = bf16[392,1536]{1,0:T(8,128)(2,1)} collective-permute-done((bf16[392,1536]{1,0:T(8,128)(2,1)}, bf16[392,1536]{1,0:T(8,128)(2,1)}, u32[]{:S(2)}, u32[]{:S(2)}) %collective-permute-start.1) | collective-permute-done | bytes 1204256 | tf_op jit(solution)/shard_map/ppermute | solution.py:28
  213.1 7.7 collective-permute-done.2
  220.8 118.1 %conditional.7 = (bf16[392,1536]{0,1:T(8,128)(2,1)}, f32[392,768]{1,0:T(8,128)}, bf16[392,768]{1,0:T(8,128)(2,1)S(1)}, bf16[392,2304]{1,0:T(8,128)(2,1)}, bf16[3...) conditional(s32[]{:T(128)} %convert_element_type.352, ...), branch_computations={%region_42.65_spmd, %region_65.84_spmd} | conditional | flops 12794345472 | bytes 326154624 | solution.py:423
  224.6 3.8 convolution_convert_fusion.20
  230.6 2.6 copy.413
  239.7 2.9 copy.412
  253.3 3.9 multiply_convert_fusion.37
  257.3 4.0 fusion.373
  261.7 4.1 multiply_reduce_fusion.30
  266.1 4.3 fusion.282
  270.4 4.6 multiply_reduce_fusion.31
  282.0 4.0 multiply_reduce_fusion.28
  291.0 3.2 reshape.863
  296.2 2.6 fusion.298
  300.6 2.7 reshape.864
  304.3 3.4 fusion.296
  309.9 5.2 fusion.304
  316.6 4.1 copy.428
  344.1 27.8 %collective-permute-done.5 = bf16[392,1536]{1,0:T(8,128)(2,1)} collective-permute-done((bf16[392,1536]{1,0:T(8,128)(2,1)S(1)}, bf16[392,1536]{1,0:T(8,128)(2,1)}, u32[]{:S(2)}, u32[]{:S(2)}) %collective-permute-start.5) | collective-permute-done | bytes 1204256 | tf_op jit(solution)/shard_map/ppermute | solution.py:28
  371.9 95.1 %conditional.8 = (f32[392,768]{1,0:T(8,128)}, bf16[392,768]{1,0:T(8,128)(2,1)S(1)}, bf16[392,2304]{0,1:T(8,128)(2,1)}, bf16[392,768]{0,1:T(8,128)(2,1)}, bf16[39...) conditional(s32[]{:T(128)} %convert_element_type.352, () %tuple.54, ...), branch_computations={%region_84.85_spmd, %region_85.104_spmd} | conditional | flops 12794345472 | bytes 276106112 | solution.py:423
  372.7 3.8 convolution_convert_fusion.24
  387.6 2.9 copy.438
  401.1 4.0 multiply_convert_fusion.43
  405.1 4.0 fusion.376
  409.5 4.0 multiply_reduce_fusion.41
  413.9 4.3 fusion.316
  418.2 4.6 multiply_reduce_fusion.42
  427.3 2.7 copy.443
  430.0 4.0 multiply_reduce_fusion.39
  438.9 3.2 reshape.871
  444.2 2.6 fusion.332
  452.0 3.4 fusion.330
  457.6 5.2 fusion.338
  467.0 54.6 %conditional.9 = (f32[768,2304]{1,0:T(8,128)}, f32[768,768]{1,0:T(8,128)S(1)}, f32[768,1536]{0,1:T(8,128)}, f32[768,3072]{1,0:T(8,128)}, f32[3072,768]{1,0:T(8,1...) conditional(s32[]{:T(128)} %convert_element_type.352, (bf16[256,768]{1,0:T(8,128)(2,1)}, ...), branch_computations={%region_104.105_spmd, %region_105.106_spmd} | conditional | flops 12993576960 | bytes 88080576 | solution.py:292
  478.1 2.8 copy.467
  480.9 8.5 fusion.56
  490.8 3.0 fusion.67
  493.8 6.5 fusion.60
  500.3 10.0 fusion.48
  510.3 9.9 fusion.52
  524.2 6.0 copy.469
  541.2 4.6 collective-permute-start.6
  548.6 4.3 collective-permute-done.4
  553.8 25.2 %reduce-scatter.19.cloned.1.call-done = f32[48,3]{1,0:T(8,128)} async-done(((f32[768,3]{1,0:T(8,128)}), f32[48,3]{1,0:T(8,128)}) %reduce-scatter.19.cloned.1.call-update) | async-done | bytes 592
  581.5 63.7 %reduce-scatter.11.cloned.1.call-done = f32[48,768]{1,0:T(8,128)} async-done(((f32[768,768]{1,0:T(8,128)}), f32[48,768]{1,0:T(8,128)}) %reduce-scatter.11.cloned.1.call-update) | async-done | bytes 147472 | tf_op jit(solution)/shard_map/reduce_scatter | solution.py:441
  645.3 78.5 %reduce-scatter.13.cloned.1.call-done = f32[48,1536]{1,0:T(8,128)} async-done(((f32[768,1536]{1,0:T(8,128)}), f32[48,1536]{1,0:T(8,128)}) %reduce-scatter.13.cloned.1.call-update) | async-done | bytes 294928 | tf_op jit(solution)/shard_map/reduce_scatter | solution.py:442
  723.8 93.6 %reduce-scatter.9.cloned.1.call-done = f32[48,2304]{1,0:T(8,128)} async-done(((f32[768,2304]{1,0:T(8,128)}), f32[48,2304]{1,0:T(8,128)}) %reduce-scatter.9.cloned.1.call-update) | async-done | bytes 442384 | tf_op jit(solution)/shard_map/reduce_scatter | solution.py:440
  819.5 113.3 %reduce-scatter.15.cloned.1.call-done = f32[48,3072]{1,0:T(8,128)} async-done(((f32[768,3072]{1,0:T(8,128)}), f32[48,3072]{1,0:T(8,128)}) %reduce-scatter.15.cloned.1.call-update) | async-done | bytes 589840 | tf_op jit(solution)/shard_map/reduce_scatter | solution.py:443
  932.7 116.2 %reduce-scatter.17.cloned.1.call-done = f32[192,768]{1,0:T(8,128)} async-done(((f32[3072,768]{1,0:T(8,128)}), f32[192,768]{1,0:T(8,128)}) %reduce-scatter.17.cloned.1.call-update) | async-done | bytes 589840 | tf_op jit(solution)/shard_map/reduce_scatter | solution.py:444
  (382 shorter events, 184.1 us)
Async XLA Ops:
  7.2 571.9 %reduce-scatter.19.cloned.1.call-start = ((), (), s32[]{:S(2)}) async-start(), calls=%async_computation.11 | async-start | bytes 417792
  7.9 69.2 %copy-start.98 = (f32[1,3,768]{2,1,0:T(4,128)}, f32[1,3,768]{2,1,0:T(4,128)S(1)}, u32[]{:S(2)}) copy-start(f32[1,3,768]{2,1,0:T(4,128)S(1)} %copy.608) | copy-start | bytes 27652
  7.9 69.1 %copy-start.14 = (bf16[512,768]{1,0:T(8,128)(2,1)S(1)}, bf16[512,768]{1,0:T(8,128)(2,1)}, u32[]{:S(2)}) copy-start(bf16[512,768]{1,0:T(8,128)(2,1)} %param.20) | copy-start | bytes 2359300
  7.9 69.1 %copy-start.127 = (s32[4,128]{1,0:T(4,128)S(1)}, s32[4,128]{1,0:T(4,128)}, u32[]{:S(2)}) copy-start(s32[4,128]{1,0:T(4,128)} %param.21) | copy-start | bytes 6148
  7.9 69.1 %copy-start.129 = (s32[4,4]{1,0:T(4,128)S(1)}, s32[4,4]{1,0:T(4,128)}, u32[]{:S(2)}) copy-start(s32[4,4]{1,0:T(4,128)} %param.22) | copy-start | bytes 196
  48.8 28.2 %collective-permute-start = (bf16[392,1536]{1,0:T(8,128)(2,1)}, bf16[392,1536]{1,0:T(8,128)(2,1)S(1)}, u32[]{:S(2)}, u32[]{:S(2)}) collective-permute-start(bf16[392,1536]{1,0:T(8,128)(2,1)} %get-tuple-element.1177), channel_id=1, source_target_pairs={{0,16},{1,17},{2,18},{3,19},{4,20},{5,21},{6,22},{7,23},{8,24},{9,... | collective-permute-start | bytes 3612680 | tf_op jit(solution)/shard_map/ppermute | solution.py:28
  130.3 90.5 %copy-start.105 = (f32[3,768]{1,0:T(4,128)}, f32[3,768]{1,0:T(4,128)S(1)}, u32[]{:S(2)}) copy-start(f32[3,768]{1,0:T(4,128)S(1)} %get-tuple-element.378) | copy-start | bytes 27652
  130.3 90.4 %copy-start.6 = (bf16[784,768]{1,0:T(8,128)(2,1)S(1)}, bf16[784,768]{1,0:T(8,128)(2,1)}, u32[]{:S(2)}) copy-start(bf16[784,768]{1,0:T(8,128)(2,1)} %param.19) | copy-start | bytes 3612676
  130.3 90.4 %copy-start.15 = (bf16[512,768]{1,0:T(8,128)(2,1)S(1)}, bf16[512,768]{1,0:T(8,128)(2,1)}, u32[]{:S(2)}) copy-start(bf16[512,768]{1,0:T(8,128)(2,1)} %param.20) | copy-start | bytes 2359300
  130.3 90.4 %copy-start.99 = (f32[1,3,768]{2,1,0:T(4,128)S(1)}, f32[1,3,768]{2,1,0:T(4,128)}, u32[]{:S(2)}) copy-start(f32[1,3,768]{2,1,0:T(4,128)} %copy-done.98) | copy-start | bytes 27652
  130.3 90.4 %copy-start.128 = (s32[4,128]{1,0:T(4,128)S(1)}, s32[4,128]{1,0:T(4,128)}, u32[]{:S(2)}) copy-start(s32[4,128]{1,0:T(4,128)} %param.21) | copy-start | bytes 6148
  130.4 90.4 %copy-start.130 = (s32[4,4]{1,0:T(4,128)S(1)}, s32[4,4]{1,0:T(4,128)}, u32[]{:S(2)}) copy-start(s32[4,4]{1,0:T(4,128)} %param.22) | copy-start | bytes 196
  130.4 82.7 %collective-permute-start.1 = (bf16[392,1536]{1,0:T(8,128)(2,1)}, bf16[392,1536]{1,0:T(8,128)(2,1)}, u32[]{:S(2)}, u32[]{:S(2)}) collective-permute-start(bf16[392,1536]{1,0:T(8,128)(2,1)} %get-tuple-element.346), channel_id=1, source_target_pairs={{0,16},{1,17},{2,18},{3,19},{4,20},{5,21},{6,22},{7,23},{8,24},{9,... | collective-permute-start | bytes 3612680 | tf_op jit(solution)/shard_map/ppermute | solution.py:28
  190.6 30.2 %collective-permute-start.2 = (bf16[392,1536]{1,0:T(8,128)(2,1)}, bf16[392,1536]{1,0:T(8,128)(2,1)}, u32[]{:S(2)}, u32[]{:S(2)}) collective-permute-start(bf16[392,1536]{1,0:T(8,128)(2,1)} %copy.456), channel_id=1, source_target_pairs={{16,0},{17,1},{18,2},{19,3},{20,4},{21,5},{22,6},{23,7},{24,8},{25... | collective-permute-start | bytes 3612680 | tf_op jit(solution)/shard_map/ppermute | solution.py:28
  224.6 3.9 copy-start.68
  237.6 7.1 copy-start.25
  248.9 4.3 slice-start.16
  250.2 3.0 slice-start.17
  253.0 4.3 slice-start.28
  253.2 4.0 copy-start.75
  253.3 4.0 slice-start.29
  253.3 8.4 slice-start.8
  257.3 4.4 slice-start.9
  266.1 4.3 copy-start.77
  279.5 6.5 slice-start
  282.0 4.0 slice-start.1
  289.2 7.0 copy-start.26
  309.9 5.2 copy-start.33
  316.6 4.1 copy-start.50
  320.7 3.5 copy-start.122
  320.7 3.5 copy-start.124
  332.5 5.9 copy-start.69
  332.5 5.9 copy-start.72
  342.8 29.1 %collective-permute-start.5 = (bf16[392,1536]{1,0:T(8,128)(2,1)S(1)}, bf16[392,1536]{1,0:T(8,128)(2,1)}, u32[]{:S(2)}, u32[]{:S(2)}) collective-permute-start(bf16[392,1536]{1,0:T(8,128)(2,1)S(1)} %copy.458), channel_id=1, source_target_pairs={{16,0},{17,1},{18,2},{19,3},{20,4},{21,5},{22,6},{23,7},{24,8},{25... | collective-permute-start | bytes 3612680 | tf_op jit(solution)/shard_map/ppermute | solution.py:28
  372.7 4.0 copy-start.80
  385.5 7.1 copy-start.27
  396.6 4.4 slice-start.18
  400.8 4.3 slice-start.30
  401.0 4.1 copy-start.86
  401.0 4.1 slice-start.31
  401.1 8.4 slice-start.10
  405.1 4.4 slice-start.11
  413.9 4.3 copy-start.88
  427.3 6.7 slice-start.2
  430.0 4.0 slice-start.3
  437.2 7.0 copy-start.28
  457.6 5.2 copy-start.34
  462.8 3.9 copy-start.123
  462.8 3.9 copy-start.125
  462.8 4.0 copy-start.81
  462.9 4.0 copy-start.84
  493.8 6.6 copy-start.76
  493.8 6.6 copy-start.87
  500.3 10.0 copy-start.78
  500.3 10.0 copy-start.89
  510.3 10.5 copy-start.103
  523.4 121.8 %reduce-scatter.11.cloned.1.call-start = ((), (), s32[]{:S(2)}) async-start(), calls=%async_computation.7 | async-start | bytes 2506752 | tf_op jit(solution)/shard_map/reduce_scatter | solution.py:441
  524.2 199.6 %reduce-scatter.13.cloned.1.call-start = ((), (), s32[]{:S(2)}) async-start(), calls=%async_computation.8 | async-start | bytes 5013504 | tf_op jit(solution)/shard_map/reduce_scatter | solution.py:442
  530.3 287.0 %reduce-scatter.9.cloned.1.call-start = ((), (), s32[]{:S(2)}) async-start(), calls=%async_computation.6 | async-start | bytes 7520256 | tf_op jit(solution)/shard_map/reduce_scatter | solution.py:440
  530.9 401.9 %reduce-scatter.15.cloned.1.call-start = ((), (), s32[]{:S(2)}) async-start(), calls=%async_computation.9 | async-start | bytes 10027008 | tf_op jit(solution)/shard_map/reduce_scatter | solution.py:443
  531.5 517.5 %reduce-scatter.17.cloned.1.call-start = ((), (), s32[]{:S(2)}) async-start(), calls=%async_computation.10 | async-start | bytes 10027008 | tf_op jit(solution)/shard_map/reduce_scatter | solution.py:444
  533.8 13.9 %collective-permute-start.3 = (bf16[512,384]{1,0:T(8,128)(2,1)S(1)}, bf16[512,384]{1,0:T(8,128)(2,1)S(1)}, u32[]{:S(2)}, u32[]{:S(2)}) collective-permute-start(bf16[512,384]{1,0:T(8,128)(2,1)S(1)} %slice.441), channel_id=1, source_target_pairs={{16,0},{17,1},{18,2},{19,3},{20,4},{21,5},{22,6},{23,7},{24,8},{25... | collective-permute-start | bytes 1179656 | tf_op jit(solution)/shard_map/ppermute | solution.py:28
  536.3 16.6 %collective-permute-start.4 = (bf16[512,384]{1,0:T(8,128)(2,1)S(1)}, bf16[512,384]{1,0:T(8,128)(2,1)S(1)}, u32[]{:S(2)}, u32[]{:S(2)}) collective-permute-start(bf16[512,384]{1,0:T(8,128)(2,1)S(1)} %slice.440), channel_id=1, source_target_pairs={{16,0},{17,1},{18,2},{19,3},{20,4},{21,5},{22,6},{23,7},{24,8},{25... | collective-permute-start | bytes 1179656 | tf_op jit(solution)/shard_map/ppermute | solution.py:28
  541.2 39.2 %collective-permute-start.6 = (bf16[784,384]{1,0:T(8,128)(2,1)}, bf16[784,384]{1,0:T(8,128)(2,1)S(1)}, u32[]{:S(2)}, u32[]{:S(2)}) collective-permute-start(bf16[784,384]{1,0:T(8,128)(2,1)} %slice.439), channel_id=1, source_target_pairs={{0,16},{1,17},{2,18},{3,19},{4,20},{5,21},{6,22},{7,23},{8,24},{9,... | collective-permute-start | bytes 1806344 | tf_op jit(solution)/shard_map/ppermute | solution.py:28
  (29 other events, 49.1 us)
Sparse Core Ops, SparseCore 0:
  523.6 55.4 reduce-scatter.18
  583.3 61.9 reduce-scatter.10
  649.1 74.5 reduce-scatter.12
  728.1 89.1 reduce-scatter.8
  821.8 110.8 reduce-scatter.14
  937.8 111.0 reduce-scatter.16
where the time goes:
time: 1070 us; the launch traced here: 1060 us
  waiting for transfers between devices  583 us (54%)
  matrix products  179 us (17%)
  local copies, waits for them, and re-layouts  165 us (15%)
  starting transfers between devices  69 us (6%)
  other arithmetic  28.4 us (3%)
  loops' own time  17.5 us (2%)
  between operations  14.8 us (1%)
    reduce_scatter x1, waiting for transfers between devices, local(): lax.psum_scatter(all_parts[4], 'dp', scatter_dimension=0, tiled=True)  116 us
    reduce_scatter x1, waiting for transfers between devices, local(): lax.psum_scatter(all_parts[3], 'dp', scatter_dimension=0, tiled=True)  113 us
    reduce_scatter x1, waiting for transfers between devices, local(): lax.psum_scatter(all_parts[0], 'dp', scatter_dimension=0, tiled=True)  93.6 us
    ppermute x7, waiting for transfers between devices, shifted(): return lax.ppermute(block, axis, route)  89.7 us
    reduce_scatter x1, waiting for transfers between devices, local(): lax.psum_scatter(all_parts[2], 'dp', scatter_dimension=0, tiled=True)  78.5 us
    ppermute x7, starting transfers between devices, shifted(): return lax.ppermute(block, axis, route)  68.8 us
    dot_general x16, matrix products, matmul(): return jnp.dot(left_side, right_side, preferred_element_type=jnp.float32)  65.8 us
    reduce_scatter x1, waiting for transfers between devices, local(): lax.psum_scatter(all_parts[1], 'dp', scatter_dimension=0, tiled=True)  63.7 us
  transfers between devices with their start and end apart: 13, of which 12 were waited for; matrix products, arithmetic and copies ran while one was open for 2% of the time, Pallas kernels for 0%

commit v1 on v0

--- a/solution.py
+++ b/solution.py
@@ -1,6 +1,10 @@
+import functools
+
 import jax
 import jax.numpy as jnp
 from jax import lax
+from jax.experimental import pallas as pl
+from jax.experimental.pallas import tpu as pltpu
 from jax.sharding import PartitionSpec as P
 
 D = 768
@@ -20,6 +24,156 @@
 MASKED = -1e30
 ROOT_HALF = 0.7071067811865476
 INV_ROOT_TWO_PI = 0.3989422804014327
+
+
+MESH = pl.DeviceIdType.MESH
+CHUNK_COLS = 256
+GAIN_STEPS = 4
+LAG = 2
+MIB = 1 << 20
+
+
+def butterfly_partner(dp, weight):
+    return dp + weight * (1 - 2 * ((dp // weight) % 2))
+
+
+def rs_kernel(n_bits, blocks, lag, *refs):
+    n_src = len(blocks)
+    sources = refs[:n_src]
+    gains_ref = refs[n_src]
+    out_ref, gains_out = refs[n_src + 1], refs[n_src + 2]
+    own, recv_core = refs[n_src + 3], refs[n_src + 4]
+    recv = refs[n_src + 5 : n_src + 5 + n_bits - 1]
+    (gain_sum, gain_in, own_sem, send_sem, recv_sem, gain_send, gain_recv) = refs[
+        n_src + 5 + n_bits - 1 :
+    ]
+    dp = lax.axis_index("dp")
+    bits = [(dp // (1 << b)) % 2 for b in range(n_bits)]
+    partners = [butterfly_partner(dp, 1 << b) for b in range(n_bits)]
+    barrier = pltpu.get_barrier_semaphore()
+    for b in range(n_bits):
+        pl.semaphore_signal(barrier, inc=1, device_id={"dp": partners[b]}, device_id_type=MESH)
+    pl.semaphore_wait(barrier, n_bits)
+
+    rows = own.shape[-2]
+    lead = (slice(None),) * (n_bits - 1)
+    total = sum(count for count, _ in blocks)
+
+    def own_copy(src, index):
+        return pltpu.make_async_copy(src, own.at[index], own_sem.at[index])
+
+    def core_copy(src, index):
+        return pltpu.make_async_remote_copy(
+            src_ref=src, dst_ref=recv_core.at[index], send_sem=send_sem.at[0, index],
+            recv_sem=recv_sem.at[0, index], device_id={"dp": partners[0]}, device_id_type=MESH)
+
+    def gain_copy(b):
+        return pltpu.make_async_remote_copy(
+            src_ref=gain_sum.at[b], dst_ref=gain_in.at[b], send_sem=gain_send.at[b],
+            recv_sem=gain_recv.at[b], device_id={"dp": partners[b]}, device_id_type=MESH)
+
+    gain_sum[0] = gains_ref[...]
+    gain_copy(0).start()
+
+    base = 0
+    for source, (count, col_blocks) in zip(sources, blocks):
+        def launch(i, carry, source=source, base=base, col_blocks=col_blocks):
+            row = pl.multiple_of((i // col_blocks) * rows, rows)
+            col = pl.multiple_of((i % col_blocks) * CHUNK_COLS, CHUNK_COLS)
+            part = (pl.ds(row, rows), pl.ds(col, CHUNK_COLS))
+            core_copy(source.at[lead + (1 - bits[0],) + part], base + i).start()
+            own_copy(source.at[lead + (bits[0],) + part], base + i).start()
+            return carry
+        lax.fori_loop(0, count, launch, 0)
+        base += count
+
+    def stage_copy(stage, index):
+        held = own if stage == 1 else recv[stage - 2]
+        keep = (slice(None),) * (n_bits - 1 - stage)
+        return pltpu.make_async_remote_copy(
+            src_ref=held.at[(index,) + keep + (1 - bits[stage],)], dst_ref=recv[stage - 1].at[index],
+            send_sem=send_sem.at[stage, index], recv_sem=recv_sem.at[stage, index],
+            device_id={"dp": partners[stage]}, device_id_type=MESH)
+
+    def src_any(index):
+        return sources[0].at[lead + (bits[0], pl.ds(0, rows), pl.ds(0, CHUNK_COLS))]
+
+    def body(i, carry):
+        for stage in range(n_bits):
+            j = i - stage * lag
+            @pl.when((j >= 0) & (j < total))
+            def _(stage=stage, j=j):
+                f32 = jnp.float32
+                if stage == 0:
+                    own_copy(src_any(j), j).wait()
+                    core_copy(src_any(j), j).wait()
+                    own[j] = (own[j].astype(f32) + recv_core[j].astype(f32)).astype(jnp.bfloat16)
+                else:
+                    stage_copy(stage, j).wait()
+                    held = own if stage == 1 else recv[stage - 2]
+                    keep = (slice(None),) * (n_bits - 1 - stage)
+                    mine = held[(j,) + keep + (bits[stage],)].astype(f32)
+                    summed = mine + recv[stage - 1][j].astype(f32)
+                    if stage == n_bits - 1:
+                        out_ref[j] = summed
+                    else:
+                        recv[stage - 1][j] = summed.astype(jnp.bfloat16)
+                if stage < n_bits - 1:
+                    stage_copy(stage + 1, j).start()
+        for b in range(n_bits):
+            @pl.when(i == GAIN_STEPS * (b + 1))
+            def _(b=b):
+                gain_copy(b).wait()
+                summed = gain_sum[b] + gain_in[b]
+                if b == n_bits - 1:
+                    gains_out[...] = summed
+                else:
+                    gain_sum[b + 1] = summed
+                    gain_copy(b + 1).start()
+        return carry
+
+    lax.fori_loop(0, total + (n_bits - 1) * lag, body, 0)
+
+
+def reduce_scatter(sources, gains, n_dp):
+    n_bits = n_dp.bit_length() - 1
+    rows = min(source.shape[0] for source in sources) // n_dp
+    shaped, blocks = [], []
+    for source in sources:
+        share = source.shape[0] // n_dp
+        shaped.append(source.reshape((2,) * n_bits + (share, source.shape[1])))
+        col_blocks = source.shape[1] // CHUNK_COLS
+        blocks.append(((share // rows) * col_blocks, col_blocks))
+    total = sum(count for count, _ in blocks)
+    low = jnp.bfloat16
+    half = (2,) * (n_bits - 1)
+    scratch = [pltpu.VMEM((total,) + half + (rows, CHUNK_COLS), low)] * 2
+    scratch += [pltpu.VMEM((total,) + half[b:] + (rows, CHUNK_COLS), low) for b in range(1, n_bits)]
+    scratch += [
+        pltpu.VMEM((n_bits,) + gains.shape, jnp.float32),
+        pltpu.VMEM((n_bits,) + gains.shape, jnp.float32),
+        pltpu.SemaphoreType.DMA((total,)),
+        pltpu.SemaphoreType.DMA((n_bits, total)),
+        pltpu.SemaphoreType.DMA((n_bits, total)),
+        pltpu.SemaphoreType.DMA((n_bits,)),
+        pltpu.SemaphoreType.DMA((n_bits,)),
+    ]
+    any_spec = pl.BlockSpec(memory_space=pl.ANY)
+    vmem_spec = pl.BlockSpec(memory_space=pltpu.VMEM)
+    return pl.pallas_call(
+        functools.partial(rs_kernel, n_bits, tuple(blocks), LAG),
+        name="share_sums",
+        out_shape=(
+            jax.ShapeDtypeStruct((total, rows, CHUNK_COLS), jnp.float32),
+            jax.ShapeDtypeStruct(gains.shape, jnp.float32),
+        ),
+        in_specs=[any_spec] * len(sources) + [vmem_spec],
+        out_specs=(vmem_spec, vmem_spec),
+        scratch_shapes=scratch,
+        compiler_params=pltpu.CompilerParams(
+            collective_id=0, has_side_effects=True, vmem_limit_bytes=48 * MIB
+        ),
+    )(*shaped, gains)
 
 
 def shifted(block, axis, distance):
@@ -307,6 +461,34 @@
 
 def pass_down(grad_context):
     return shifted(grad_context, "section", -1)
+
+
+def chunk_columns(chunks, rows, columns):
+    col_blocks = columns // CHUNK_COLS
+    shaped = chunks.reshape(rows // chunks.shape[1], col_blocks, chunks.shape[1], CHUNK_COLS)
+    return shaped.transpose(0, 2, 1, 3).reshape(rows, columns)
+
+
+def summed_shares(attn_part, in_part, out_part, gains):
+    n_dp = lax.axis_size("dp")
+    share_rows = D // n_dp
+    if n_dp & (n_dp - 1) or share_rows % 16:
+        wide = [part.astype(jnp.float32) for part in (attn_part, in_part, out_part)]
+        sums = [lax.psum_scatter(part, "dp", scatter_dimension=0, tiled=True) for part in wide]
+        return (*sums, lax.psum_scatter(gains, "dp", scatter_dimension=1, tiled=True))
+    padded = jnp.pad(gains, ((0, 8 - gains.shape[0]), (0, 0)))
+    chunks, gain_sums = reduce_scatter([attn_part, in_part, out_part], padded, n_dp)
+    counts = [part.size // n_dp // (share_rows * CHUNK_COLS) for part in (attn_part, in_part)]
+    first, second = counts[0], counts[0] + counts[1]
+    own_gains = lax.dynamic_slice_in_dim(
+        gain_sums[: gains.shape[0]], lax.axis_index("dp") * share_rows, share_rows, 1
+    )
+    return (
+        chunk_columns(chunks[:first], share_rows, attn_part.shape[1]),
+        chunk_columns(chunks[first:second], share_rows, in_part.shape[1]),
+        chunk_columns(chunks[second:], out_part.shape[0] // n_dp, out_part.shape[1]),
+        own_gains,
+    )
 
 
 def local(patches, captions, segments, seg_images, attn_w, w_in, w_out, norm_gains, cotangent):
@@ -436,15 +618,10 @@
         if dec_on:
             grad_in = pass_down(send_down)
     all_parts = weight_pass(is_first, enc_list, dec_list)
-    shares = (
-        lax.psum_scatter(all_parts[0], "dp", scatter_dimension=0, tiled=True),
-        lax.psum_scatter(all_parts[1], "dp", scatter_dimension=0, tiled=True),
-        lax.psum_scatter(all_parts[2], "dp", scatter_dimension=0, tiled=True),
-        lax.psum_scatter(all_parts[3], "dp", scatter_dimension=0, tiled=True),
-        lax.psum_scatter(all_parts[4], "dp", scatter_dimension=0, tiled=True),
-        lax.psum_scatter(all_parts[5], "dp", scatter_dimension=1, tiled=True),
-    )
-    attn_share = jnp.concatenate([shares[0], shares[1], shares[2]], 1)
+    attn_part = jnp.concatenate(all_parts[:3], 1).astype(low_kind)
+    attn_share, in_share, out_share, gain_share = summed_shares(
+        attn_part, all_parts[3].astype(low_kind), all_parts[4].astype(low_kind), all_parts[5]
+    )
     patch_grad = jnp.concatenate(patch_rows_list, 0)
     decoded = jnp.concatenate(decoded_list, 0)
     caption_grad = jnp.concatenate(caption_rows_list, 0)
@@ -466,9 +643,9 @@
         caption_out,
         patch_out,
         attn_share[None],
-        shares[3][None],
-        shares[4][None],
-        shares[5][None],
+        in_share[None],
+        out_share[None],
+        gain_share[None],
     )
 
 

time: 1070 us -> 668 us (0.62)
  waiting for transfers between devices: 583 us -> 87.7 us
  Pallas kernels: 0 us -> 105 us
  between operations: 14.8 us -> 1.4 us
    reduce_scatter x5 -> x0, waiting for transfers between devices: 465 us -> none  [the longest x1 116 us: local(): lax.psum_scatter(all_parts[4], 'dp', scatter_dimension=0, tiled=True)]
    pallas_call x0 -> x1, Pallas kernels: none -> 105 us  [reduce_scatter(): pl.pallas_call(functools.partial(rs_kernel, n_bits, tuple(blocks), LAG),...]
    unnamed x7 -> x0, waiting for transfers between devices: 27.5 us -> none
    cond x139 -> x92, local copies, waits for them, and re-layouts: 30.2 us -> 22.2 us
    another operation x32 -> x35, local copies, waits for them, and re-layouts: 33.7 us -> 36.9 us
  transfers between devices with their start and end apart: 13 -> 7, of which waited for: 12 -> 5; matrix products, arithmetic and copies ran while one was open for 2% -> 10% of each run, Pallas kernels for 0% -> 16%
where the time goes in v1:
time: 668 us; the launch traced here: 656 us
  matrix products  181 us (27%)
  local copies, waits for them, and re-layouts  164 us (25%)
  Pallas kernels  105 us (16%)
  waiting for transfers between devices  87.7 us (13%)
  starting transfers between devices  66.2 us (10%)
  other arithmetic  38.7 us (6%)
  loops' own time  11.7 us (2%)
    pallas_call x1, Pallas kernels, reduce_scatter(): pl.pallas_call(functools.partial(rs_kernel, n_bits, tuple(blocks), LAG),...  105 us
    ppermute x7, waiting for transfers between devices, shifted(): return lax.ppermute(block, axis, route)  87.7 us
    dot_general x16, matrix products, matmul(): return jnp.dot(left_side, right_side, preferred_element_type=jnp.float32)  68.6 us
    ppermute x7, starting transfers between devices, shifted(): return lax.ppermute(block, axis, route)  66.2 us
    dot_general x10, matrix products, matmul_nt(): lax.dot_general(left_side, right_side, (((1,), (1,)), ((), ())), preferre...  41.8 us
    reshape x18, local copies, waits for them, and re-layouts, split_three(): qkv_low[:, index * D:(index + 1) * D].reshape(head_shape)  38.7 us
    another operation x32, local copies, waits for them, and re-layouts  33.8 us
    dot_general x5, matrix products, matmul_tn(): lax.dot_general(left_side, right_side, (((0,), (0,)), ((), ())), preferre...  33.2 us
  transfers between devices with their start and end apart: 7, of which 5 were waited for; matrix products, arithmetic and copies ran while one was open for 10% of the time, Pallas kernels for 16%

profile of v1, /device:TPU:0, one launch (start us, length us, event | category | flops | bytes accessed | tf_op | source)
XLA Modules:
  0.0 656.1 jit_solution(15164431895645422944)
XLA Ops:
  1.4 40.9 %conditional.5 = (bf16[392,1536]{1,0:T(8,128)(2,1)}) conditional(s32[]{:T(128)} %convert_element_type.362, () %tuple.54, (bf16[784,768]{1,0:T(8,128)(2,1)}, f32[3,768]{1,0:T(4,128)S(1)}, bf16[768,4608]{1,0:T(8,128)(2,1)}, bf16[768,3072]{1,0:T(8,128)(2,1)}, bf16[3072,768]{1,0:T(8,128)(2,1)}) %tuple.242), branch_computations={%region_0.0_spmd, %region_1.0_spmd} | conditional | flops 6734167552 | bytes 77639224 | solution.py:605
  4.1 3.9 convolution_convert_fusion.5
  11.4 3.0 reshape.911
  14.4 2.5 multiply_reduce_fusion
  20.1 3.5 fusion.93
  29.0 8.8 %fusion.352 = (f32[392]{0:T(512)S(1)}, f32[392,768]{1,0:T(8,128)S(1)}) fusion(f32[392,768]{1,0:T(8,128)} %copy-done.64, bf16[3072,768]{1,0:T(8,128)(2,1)} %get-tuple-element.187, bf16[768,3072]{1,0:T(8,128)(2,1)} %get-tuple-element.186, f32[768]{0:T(1024)S(1)} %get-tuple-element.847, f32[392]{0:T(512)S(1)} %add_rsqrt_fusion.1, ...), kind=kOutput, calls=%fused_computation.664 | convolution fusion | flops 3707203072 | bytes 11853408 | tf_op jit(solution)/shard_map/cond/branch_1_fun/dot_general | solution.py:186
  38.1 3.9 convolution_convert_fusion.6
  43.7 26.9 %collective-permute-done = bf16[392,1536]{1,0:T(8,128)(2,1)S(1)} collective-permute-done((bf16[392,1536]{1,0:T(8,128)(2,1)}, bf16[392,1536]{1,0:T(8,128)(2,1)S(1)}, u32[]{:S(2)}, u32[]{:S(2)}) %collective-permute-start) | collective-permute-done | bytes 1204256 | tf_op jit(solution)/shard_map/ppermute | solution.py:182
  70.5 53.3 %conditional.6 = (bf16[392,1536]{1,0:T(8,128)(2,1)}, bf16[392,1536]{0,1:T(8,128)(2,1)}, f32[256,768]{1,0:T(8,128)}, f32[256,768]{1,0:T(8,128)}, bf16[256,768]{1,...) conditional(s32[]{:T(128)} %convert_element_type.362, ...), branch_computations={%region_10.33_spmd, %region_33.42_spmd} | conditional | flops 9754902528 | bytes 296949408 | solution.py:605
  76.1 3.9 convolution_convert_fusion.15
  82.0 2.7 reshape.914
  88.9 3.5 fusion.188
  96.8 8.8 %fusion.355 = (f32[392]{0:T(512)S(1)}, f32[392,768]{1,0:T(8,128)S(1)}) fusion(f32[392,768]{1,0:T(8,128)} %copy-done.65, bf16[3072,768]{1,0:T(8,128)(2,1)} %get-tuple-element.201, bf16[768,3072]{1,0:T(8,128)(2,1)} %get-tuple-element.200, f32[768]{0:T(1024)S(1)} %get-tuple-element.862, f32[392]{0:T(512)S(1)} %add_rsqrt_fusion.7, ...), kind=kOutput, calls=%fused_computation.667 | convolution fusion | flops 3707203072 | bytes 11853408 | tf_op jit(solution)/shard_map/cond/branch_1_fun/dot_general | solution.py:186
  105.8 3.9 convolution_convert_fusion.16
  124.0 57.6 %collective-permute-start.1 = (bf16[392,1536]{1,0:T(8,128)(2,1)}, bf16[392,1536]{1,0:T(8,128)(2,1)}, u32[]{:S(2)}, u32[]{:S(2)}) collective-permute-start(bf16[392,1536]{1,0:T(8,128)(2,1)} %get-tuple-element.344), channel_id=1, source_target_pairs={{0,16},{1,17},{2,18},{3,19},{4,20},{5,21},{6,22},{7,23},{8,24},{9,... | collective-permute-start | bytes 3612680 | tf_op jit(solution)/shard_map/ppermute | solution.py:182
  181.6 2.5 copy.460
  185.4 21.3 %collective-permute-done.1 = bf16[392,1536]{1,0:T(8,128)(2,1)} collective-permute-done((bf16[392,1536]{1,0:T(8,128)(2,1)}, bf16[392,1536]{1,0:T(8,128)(2,1)}, u32[]{:S(2)}, u32[]{:S(2)}) %collective-permute-start.1) | collective-permute-done | bytes 1204256 | tf_op jit(solution)/shard_map/ppermute | solution.py:182
  206.6 7.7 %collective-permute-done.2 = bf16[392,1536]{1,0:T(8,128)(2,1)} collective-permute-done((bf16[392,1536]{1,0:T(8,128)(2,1)}, bf16[392,1536]{1,0:T(8,128)(2,1)}, u32[]{:S(2)}, u32[]{:S(2)}) %collective-permute-start.2) | collective-permute-done | bytes 1204256 | tf_op jit(solution)/shard_map/ppermute | solution.py:182
  214.3 123.8 %conditional.7 = (bf16[392,1536]{0,1:T(8,128)(2,1)}, f32[392,768]{1,0:T(8,128)}, bf16[392,768]{1,0:T(8,128)(2,1)}, bf16[392,2304]{1,0:T(8,128)(2,1)}, bf16[392,7...) conditional(s32[]{:T(128)} %convert_element_type.362, ...), branch_computations={%region_42.65_spmd, %region_65.84_spmd} | conditional | flops 12794345472 | bytes 326154528 | solution.py:605
  219.0 3.8 convolution_convert_fusion.25
  225.0 2.6 copy.417
  234.1 2.9 copy.416
  244.4 2.4 fusion.367
  248.2 5.3 multiply_convert_fusion.37
  253.6 4.0 fusion.368
  258.0 4.0 multiply_reduce_fusion.30
  263.3 5.3 fusion.277
  268.6 4.6 multiply_reduce_fusion.31
  278.7 2.5 copy.421
  281.2 4.0 multiply_reduce_fusion.28
  290.2 3.2 reshape.883
  295.5 2.6 fusion.293
  299.8 2.7 reshape.884
  303.5 3.4 fusion.291
  309.2 5.2 fusion.299
  315.9 4.2 copy.432
  338.2 2.5 copy.462
  354.0 26.6 %collective-permute-done.3 = bf16[512,384]{1,0:T(8,128)(2,1)S(1)} collective-permute-done((bf16[512,384]{1,0:T(8,128)(2,1)S(1)}, bf16[512,384]{1,0:T(8,128)(2,1)S(1)}, u32[]{:S(2)}, u32[]{:S(2)}) %collective-permute-start.3) | collective-permute-done | bytes 393248 | tf_op jit(solution)/shard_map/ppermute | solution.py:182
  381.4 5.3 collective-permute-done.4
  387.6 100.5 %conditional.8 = (f32[392,768]{1,0:T(8,128)S(1)}, bf16[392,768]{1,0:T(8,128)(2,1)}, bf16[392,2304]{0,1:T(8,128)(2,1)}, bf16[392,768]{0,1:T(8,128)(2,1)}, bf16[39...) conditional(s32[]{:T(128)} %convert_element_type.362, () %tuple.59, ...), branch_computations={%region_84.85_spmd, %region_85.104_spmd} | conditional | flops 12794345472 | bytes 261655232 | solution.py:605
  389.3 3.8 convolution_convert_fusion.29
  404.1 2.9 copy.442
  418.4 5.4 multiply_convert_fusion.43
  423.8 4.0 fusion.371
  428.2 4.0 multiply_reduce_fusion.41
  433.4 5.3 fusion.311
  438.8 4.6 multiply_reduce_fusion.42
  448.9 2.7 copy.447
  451.6 4.0 multiply_reduce_fusion.39
  460.6 3.2 reshape.891
  465.9 2.6 fusion.327
  470.2 2.5 reshape.892
  473.7 3.4 fusion.325
  479.3 5.2 fusion.333
  489.3 2.4 slice.457
  493.8 42.9 %conditional.9 = (bf16[768,3072]{1,0:T(8,128)(2,1)}, bf16[3072,768]{1,0:T(8,128)(2,1)}, bf16[2,2,2,2,48,2304]{5,4,3,2,1,0:T(8,128)(2,1)}, bf16[2,2,2,2,48,768]{5...) conditional(s32[]{:T(128)} %convert_element_type.362, ...), branch_computations={%region_104.105_spmd, %region_105.106_spmd} | conditional | flops 12997115904 | bytes 51118136 | solution.py:446
  497.2 9.4 %fusion.46 = bf16[768,3072]{1,0:T(8,128)(2,1)} fusion(bf16[392,3072]{1,0:T(8,128)(2,1)} %get-tuple-element.252, bf16[392,3072]{1,0:T(8,128)(2,1)} %get-tuple-element.251, bf16[392,768]{1,0:T(8,128)(2,1)} %get-tuple-element.250, bf16[392,768]{1,0:T(8,128)(2,1)} %get-tuple-element.249), kind=kOutput, calls=%fused_computation.50 | convolution fusion | flops 3711418368 | bytes 10739712 | tf_op jit(solution)/shard_map/cond/branch_1_fun/dot_general | solution.py:196
  506.6 8.7 %fusion.50 = bf16[3072,768]{1,0:T(8,128)(2,1)} fusion(bf16[392,3072]{1,0:T(8,128)(2,1)} %get-tuple-element.254, bf16[392,3072]{1,0:T(8,128)(2,1)} %get-tuple-element.253, bf16[392,768]{1,0:T(8,128)(2,1)} %get-tuple-element.256, bf16[392,768]{1,0:T(8,128)(2,1)} %get-tuple-element.255), kind=kOutput, calls=%fused_computation.54 | convolution fusion | flops 3711418368 | bytes 10739712 | tf_op jit(solution)/shard_map/cond/branch_1_fun/dot_general | solution.py:196
  515.4 2.8 copy.471
  518.1 7.5 %convolution_convert_fusion.2 = bf16[768,2304]{1,0:T(8,128)(2,1)} fusion(bf16[392,2304]{1,0:T(8,128)(2,1)S(1)} %copy.471, bf16[392,2304]{1,0:T(8,128)(2,1)} %get-tuple-element.259, bf16[392,768]{1,0:T(8,128)(2,1)} %get-tuple-element.258, bf16[392,768]{1,0:T(8,128)(2,1)} %get-tuple-element.257), kind=kOutput, calls=%fused_computation.49 | convolution fusion | flops 2785935360 | bytes 8355840 | tf_op jit(solution)/shard_map/cond/branch_1_fun/dot_general | solution.py:196
  527.0 2.9 convolution_convert_fusion.4
  529.9 4.7 convolution_convert_fusion.3
  537.5 6.5 pad_maximum_fusion.6.refs_0_
  544.0 105.0 %share_sums.1 = (f32[42,48,256]{2,1,0:T(8,128)S(1)}, f32[8,768]{1,0:T(8,128)S(1)}) custom-call(bf16[2,2,2,2,48,4608]{5,4,3,2,1,0:T(8,128)(2,1)} %pad_maximum_fusion.6.refs_0_, bf16[2,2,2,2,48,3072]{5,4,3,2,1,0:T(8,128)(2,1)S(1)} %bitcast.334, bf16[2,2,2,2,192,768]{5,4,3,2,1,0:T(8,128)(2,1)S(1)} %bitcast.337, f32[8,768]{1,0:T(8,128)S(1)} %pad.6.refs_3_), custom_call_target="tpu_custom_call" | custom-call | tf_op jit(solution)/shard_map/share_sums/pallas_call | solution.py:163
  (335 shorter events, 178.0 us)
Async XLA Ops:
  1.3 69.2 %copy-start.67 = (f32[1,3,768]{2,1,0:T(4,128)}, f32[1,3,768]{2,1,0:T(4,128)S(1)}, u32[]{:S(2)}) copy-start(f32[1,3,768]{2,1,0:T(4,128)S(1)} %copy.614) | copy-start | bytes 27652
  1.3 69.2 %copy-start.14 = (bf16[512,768]{1,0:T(8,128)(2,1)S(1)}, bf16[512,768]{1,0:T(8,128)(2,1)}, u32[]{:S(2)}) copy-start(bf16[512,768]{1,0:T(8,128)(2,1)} %param.20) | copy-start | bytes 2359300
  1.3 69.2 %copy-start.94 = (s32[4,128]{1,0:T(4,128)S(1)}, s32[4,128]{1,0:T(4,128)}, u32[]{:S(2)}) copy-start(s32[4,128]{1,0:T(4,128)} %param.21) | copy-start | bytes 6148
  1.4 69.2 %copy-start.96 = (s32[4,4]{1,0:T(4,128)S(1)}, s32[4,4]{1,0:T(4,128)}, u32[]{:S(2)}) copy-start(s32[4,4]{1,0:T(4,128)} %param.22) | copy-start | bytes 196
  16.9 2.2 copy-start.4
  23.5 2.1 copy-start.7
  42.3 28.2 %collective-permute-start = (bf16[392,1536]{1,0:T(8,128)(2,1)}, bf16[392,1536]{1,0:T(8,128)(2,1)S(1)}, u32[]{:S(2)}, u32[]{:S(2)}) collective-permute-start(bf16[392,1536]{1,0:T(8,128)(2,1)} %get-tuple-element.1152), channel_id=1, source_target_pairs={{0,16},{1,17},{2,18},{3,19},{4,20},{5,21},{6,22},{7,23},{8,24},{9,... | collective-permute-start | bytes 3612680 | tf_op jit(solution)/shard_map/ppermute | solution.py:182
  85.7 2.2 copy-start.5
  85.8 2.2 copy-start.55
  123.9 90.4 %copy-start.72 = (f32[3,768]{1,0:T(4,128)}, f32[3,768]{1,0:T(4,128)S(1)}, u32[]{:S(2)}) copy-start(f32[3,768]{1,0:T(4,128)S(1)} %get-tuple-element.376) | copy-start | bytes 27652
  123.9 90.4 %copy-start.6 = (bf16[784,768]{1,0:T(8,128)(2,1)S(1)}, bf16[784,768]{1,0:T(8,128)(2,1)}, u32[]{:S(2)}) copy-start(bf16[784,768]{1,0:T(8,128)(2,1)} %param.19) | copy-start | bytes 3612676
  123.9 90.4 %copy-start.15 = (bf16[512,768]{1,0:T(8,128)(2,1)S(1)}, bf16[512,768]{1,0:T(8,128)(2,1)}, u32[]{:S(2)}) copy-start(bf16[512,768]{1,0:T(8,128)(2,1)} %param.20) | copy-start | bytes 2359300
  123.9 90.4 %copy-start.68 = (f32[1,3,768]{2,1,0:T(4,128)S(1)}, f32[1,3,768]{2,1,0:T(4,128)}, u32[]{:S(2)}) copy-start(f32[1,3,768]{2,1,0:T(4,128)} %copy-done.67) | copy-start | bytes 27652
  123.9 90.4 %copy-start.95 = (s32[4,128]{1,0:T(4,128)S(1)}, s32[4,128]{1,0:T(4,128)}, u32[]{:S(2)}) copy-start(s32[4,128]{1,0:T(4,128)} %param.21) | copy-start | bytes 6148
  123.9 90.4 %copy-start.97 = (s32[4,4]{1,0:T(4,128)S(1)}, s32[4,4]{1,0:T(4,128)}, u32[]{:S(2)}) copy-start(s32[4,4]{1,0:T(4,128)} %param.22) | copy-start | bytes 196
  124.0 82.7 %collective-permute-start.1 = (bf16[392,1536]{1,0:T(8,128)(2,1)}, bf16[392,1536]{1,0:T(8,128)(2,1)}, u32[]{:S(2)}, u32[]{:S(2)}) collective-permute-start(bf16[392,1536]{1,0:T(8,128)(2,1)} %get-tuple-element.344), channel_id=1, source_target_pairs={{0,16},{1,17},{2,18},{3,19},{4,20},{5,21},{6,22},{7,23},{8,24},{9,... | collective-permute-start | bytes 3612680 | tf_op jit(solution)/shard_map/ppermute | solution.py:182
  184.1 30.2 %collective-permute-start.2 = (bf16[392,1536]{1,0:T(8,128)(2,1)}, bf16[392,1536]{1,0:T(8,128)(2,1)}, u32[]{:S(2)}, u32[]{:S(2)}) collective-permute-start(bf16[392,1536]{1,0:T(8,128)(2,1)} %copy.460), channel_id=1, source_target_pairs={{16,0},{17,1},{18,2},{19,3},{20,4},{21,5},{22,6},{23,7},{24,8},{25... | collective-permute-start | bytes 3612680 | tf_op jit(solution)/shard_map/ppermute | solution.py:182
  231.9 7.1 %copy-start.25 = (bf16[2,196,12,64]{1,3,2,0:T(8,128)(2,1)}, bf16[2,196,12,64]{1,3,2,0:T(8,128)(2,1)S(1)}, u32[]{:S(2)}) copy-start(bf16[2,196,12,64]{1,3,2,0:T(8,128)(2,1)S(1)} %copy.415) | copy-start | bytes 1806340 | tf_op jit(solution)/shard_map/cond
  239.0 2.2 copy-start
  243.1 5.1 slice-start.20
  244.4 3.8 slice-start.21
  247.1 6.4 slice-start.32
  248.2 5.4 slice-start.33
  248.2 9.8 %slice-start.12 = ((s8[7077888]{0:T(1024)(128)(4,1)}), s8[4194304]{0:T(1024)(128)(4,1)S(1)}, s32[]{:S(2)}) async-start(s8[7077888]{0:T(1024)(128)(4,1)} %bitcast.373), calls=%async_computation.12 | async-start | bytes 8388608 | tf_op jit(solution)/shard_map/cond
  253.6 4.4 slice-start.13
  278.7 6.5 slice-start
  281.2 4.0 slice-start.1
  285.2 2.7 copy-start.29
  286.4 1.5 copy-start.9
  288.5 7.0 %copy-start.26 = (bf16[2,196,12,64]{1,3,2,0:T(8,128)(2,1)S(1)}, bf16[2,196,12,64]{1,3,2,0:T(8,128)(2,1)}, u32[]{:S(2)}) copy-start(bf16[2,196,12,64]{1,3,2,0:T(8,128)(2,1)} %copy-done.25) | copy-start | bytes 1806340 | tf_op jit(solution)/shard_map/cond
  309.2 5.2 copy-start.33
  315.9 4.2 copy-start.51
  320.0 3.5 copy-start.89
  320.0 3.5 copy-start.91
  338.1 3.8 copy-start.71
  340.6 47.0 %collective-permute-start.5 = (bf16[392,1536]{1,0:T(8,128)(2,1)}, bf16[392,1536]{1,0:T(8,128)(2,1)}, u32[]{:S(2)}, u32[]{:S(2)}) collective-permute-start(bf16[392,1536]{1,0:T(8,128)(2,1)} %copy.462), channel_id=1, source_target_pairs={{16,0},{17,1},{18,2},{19,3},{20,4},{21,5},{22,6},{23,7},{24,8},{25... | collective-permute-start | bytes 3612680 | tf_op jit(solution)/shard_map/ppermute | solution.py:182
  345.6 35.0 %collective-permute-start.3 = (bf16[512,384]{1,0:T(8,128)(2,1)S(1)}, bf16[512,384]{1,0:T(8,128)(2,1)S(1)}, u32[]{:S(2)}, u32[]{:S(2)}) collective-permute-start(bf16[512,384]{1,0:T(8,128)(2,1)S(1)} %slice.459), channel_id=1, source_target_pairs={{16,0},{17,1},{18,2},{19,3},{20,4},{21,5},{22,6},{23,7},{24,8},{25... | collective-permute-start | bytes 1179656 | tf_op jit(solution)/shard_map/ppermute | solution.py:182
  349.0 37.7 %copy-start.54 = (f32[512,768]{1,0:T(8,128)S(1)}, f32[512,768]{1,0:T(8,128)}, u32[]{:S(2)}) copy-start(f32[512,768]{1,0:T(8,128)} %constant_dynamic-update-slice_fusion.8) | copy-start | bytes 4718596
  350.3 36.4 %collective-permute-start.4 = (bf16[512,384]{1,0:T(8,128)(2,1)S(1)}, bf16[512,384]{1,0:T(8,128)(2,1)S(1)}, u32[]{:S(2)}, u32[]{:S(2)}) collective-permute-start(bf16[512,384]{1,0:T(8,128)(2,1)S(1)} %slice.458), channel_id=1, source_target_pairs={{16,0},{17,1},{18,2},{19,3},{20,4},{21,5},{22,6},{23,7},{24,8},{25... | collective-permute-start | bytes 1179656 | tf_op jit(solution)/shard_map/ppermute | solution.py:182
  387.7 1.6 copy-start.78
  402.0 7.1 %copy-start.27 = (bf16[2,196,12,64]{1,3,2,0:T(8,128)(2,1)}, bf16[2,196,12,64]{1,3,2,0:T(8,128)(2,1)S(1)}, u32[]{:S(2)}) copy-start(bf16[2,196,12,64]{1,3,2,0:T(8,128)(2,1)S(1)} %copy.441) | copy-start | bytes 1806340 | tf_op jit(solution)/shard_map/cond
  409.1 2.2 copy-start.1
  413.2 5.1 slice-start.22
  414.5 3.8 slice-start.23
  417.3 6.5 slice-start.34
  418.4 5.4 slice-start.35
  418.4 9.8 %slice-start.14 = ((s8[7077888]{0:T(1024)(128)(4,1)}), s8[4194304]{0:T(1024)(128)(4,1)S(1)}, s32[]{:S(2)}) async-start(s8[7077888]{0:T(1024)(128)(4,1)} %bitcast.375), calls=%async_computation.14 | async-start | bytes 8388608 | tf_op jit(solution)/shard_map/cond
  423.8 4.4 slice-start.15
  448.9 6.7 %slice-start.2 = ((s8[4915200]{0:T(1024)(128)(4,1)}), s8[720896]{0:T(1024)(128)(4,1)S(1)}, s32[]{:S(2)}) async-start(s8[4915200]{0:T(1024)(128)(4,1)} %bitcast.320), calls=%async_computation.2 | async-start | bytes 1441792 | tf_op jit(solution)/shard_map/cond
  451.6 4.0 slice-start.3
  455.6 2.7 copy-start.30
  458.9 7.0 %copy-start.28 = (bf16[2,196,12,64]{1,3,2,0:T(8,128)(2,1)S(1)}, bf16[2,196,12,64]{1,3,2,0:T(8,128)(2,1)}, u32[]{:S(2)}) copy-start(bf16[2,196,12,64]{1,3,2,0:T(8,128)(2,1)} %copy-done.27) | copy-start | bytes 1806340 | tf_op jit(solution)/shard_map/cond
  477.1 2.2 copy-start.79
  479.3 5.2 copy-start.34
  484.5 2.9 copy-start.90
  484.5 2.8 copy-start.92
  488.1 5.7 copy-start.99
  488.2 5.7 copy-start.101
  491.7 161.7 %collective-permute-start.6 = (bf16[784,384]{1,0:T(8,128)(2,1)}, bf16[784,384]{1,0:T(8,128)(2,1)}, u32[]{:S(2)}, u32[]{:S(2)}) collective-permute-start(bf16[784,384]{1,0:T(8,128)(2,1)} %slice.457), channel_id=1, source_target_pairs={{0,16},{1,17},{2,18},{3,19},{4,20},{5,21},{6,22},{7,23},{8,24},{9,... | collective-permute-start | bytes 1806344 | tf_op jit(solution)/shard_map/ppermute | solution.py:182
  537.4 6.6 %slice-start.8 = ((s8[4718592]{0:T(1024)(128)(4,1)}), s8[4194304]{0:T(1024)(128)(4,1)S(1)}, s32[]{:S(2)}) async-start(s8[4718592]{0:T(1024)(128)(4,1)} %bitcast.332), calls=%async_computation.8 | async-start | bytes 8388608
  537.4 6.6 slice-start.10
  537.4 6.6 slice-start.9
  537.5 6.6 %slice-start.11 = ((s8[4718592]{0:T(1024)(128)(4,1)}), s8[524288]{0:T(1024)(128)(4,1)S(1)}, s32[]{:S(2)}) async-start(s8[4718592]{0:T(1024)(128)(4,1)} %bitcast.335), calls=%async_computation.11 | async-start | bytes 1048576
  650.2 3.2 copy-start.35
  (4 other events, 4.8 us)

commit v2 on v0

v2 whole, which is shorter than its diff:
```python
import functools
import jax
import jax.numpy as jnp
from jax import lax
from jax.experimental import pallas as pl
from jax.experimental.pallas import tpu as pltpu
from jax.sharding import PartitionSpec as P

D = 768
FF = 3072
HEADS = 12
HEAD = 64
PATCHES = 196
ROW = 128
SEGS = 4
MICRO = 2
IMG_MB = 2
ROWS_MB = 2
NORM_EPS = 1e-06
SCORE_SCALE = 0.125
MASKED = -1e30
ROOT_HALF = 0.7071067811865476
INV_ROOT_TWO_PI = 0.3989422804014327
MESH = pl.DeviceIdType.MESH
MIB = 1 << 20

LOW = jnp.bfloat16
WIDE = jnp.float32
IMG_ROWS = -(-PATCHES // 16) * 16
ENC_MB = IMG_MB * IMG_ROWS
ENC_ROWS = MICRO * ENC_MB
DEC_MB = ROWS_MB * ROW
DEC_ROWS = MICRO * DEC_MB
PAIR = 2 * HEAD
PAIRS = HEADS // 2
HALF = D // 2
QUARTER = D // 4


def dot_nn(left, right):
    return lax.dot_general(left, right, (((1,), (0,)), ((), ())), preferred_element_type=WIDE)


def dot_nt(left, right):
    return lax.dot_general(left, right, (((1,), (1,)), ((), ())), preferred_element_type=WIDE)


def dot_tn(left, right):
    return lax.dot_general(left, right, (((0,), (0,)), ((), ())), preferred_element_type=WIDE)


def rows_at(start, size):
    return pl.ds(pl.multiple_of(start, 16), size)


def cols_at(start, size):
    return pl.ds(pl.multiple_of(start, 128), size)


def norm_hat(values):
    centred = values - jnp.mean(values, -1, keepdims=True)
    inverse = lax.rsqrt(jnp.mean(centred * centred, -1, keepdims=True) + NORM_EPS)
    return centred * inverse, inverse


def norm_low(values, gain):
    return (norm_hat(values)[0] * gain).astype(LOW)


def norm_back(upstream, values, gain):
    normed, inverse = norm_hat(values)
    scaled = upstream * gain
    inner = (
        scaled
        - jnp.mean(scaled, -1, keepdims=True)
        - normed * jnp.mean(scaled * normed, -1, keepdims=True)
    )
    return inner * inverse, jnp.sum(upstream * normed, 0, keepdims=True)


def gelu_parts(hidden):
    normal_cdf = 0.5 * (1.0 + lax.erf(hidden * ROOT_HALF))
    slope = normal_cdf + hidden * INV_ROOT_TWO_PI * jnp.exp(-0.5 * hidden * hidden)
    return hidden * normal_cdf, slope


def first_lanes(rows):
    return lax.broadcasted_iota(jnp.int32, (rows, PAIR), 1) < HEAD


def split_pair(block):
    first = (lax.broadcasted_iota(jnp.int32, (1, PAIR), 1) < HEAD).astype(WIDE)
    return jnp.concatenate([block * first.astype(LOW), block * (1.0 - first).astype(LOW)], 0)


def join_pair(stacked):
    rows = stacked.shape[0] // 2
    return jnp.where(first_lanes(rows), stacked[:rows], stacked[rows:])


def attend_pair(queries, keys, values, bias):
    stacked = split_pair(queries) * jnp.asarray(SCORE_SCALE, LOW)
    scores = dot_nt(stacked, keys) + bias
    powers = jnp.exp(scores - jnp.max(scores, -1, keepdims=True))
    chances = powers * (1.0 / jnp.sum(powers, -1, keepdims=True))
    return join_pair(dot_nn(chances.astype(LOW), values)).astype(LOW)


def attend_pair_back(queries, keys, values, grad_mixed, bias):
    stacked = split_pair(queries) * jnp.asarray(SCORE_SCALE, LOW)
    grads = split_pair(grad_mixed)
    scores = dot_nt(keys, stacked) + bias
    powers = jnp.exp(scores - jnp.max(scores, 0, keepdims=True))
    chances = powers * (1.0 / jnp.sum(powers, 0, keepdims=True))
    grad_chances = dot_nt(values, grads)
    inner = jnp.sum(grad_chances * chances, 0, keepdims=True)
    grad_scores = (chances * (grad_chances - inner)).astype(LOW)
    grad_keys = dot_nn(grad_scores, stacked)
    grad_values = dot_nn(chances.astype(LOW), grads)
    grad_queries = join_pair(dot_tn(grad_scores, keys)) * SCORE_SCALE
    return grad_queries.astype(LOW), grad_keys.astype(LOW), grad_values.astype(LOW)


def loop(count, body):
    lax.fori_loop(0, count, lambda i, carry: (body(i), carry)[1], 0)


def main_kernel(*refs):
    (
        patches, captions, segments, seg_images, attn_w, w_in, w_out, gains, cot,
        a_out, o_out, c_out, b_out, u_out, dqkv_out, g1_out, g2_out, dh_out,
        co_out, dq_out, up_out, dctx_out, gain_out, patch_own, decoded_own, caption_own, exch_out,
        wa, wi, wo, wctx, x, ct, a, o, b, c, qkv, u, slope, x1, x2, g1, g2, landed, dmix, ctx,
        co, cq, g2w, tmp, sent, bias, bias_t, exch, decoded_half,
        load_sem, out_sem, up_send, up_recv, ctx_send, ctx_recv,
    ) = refs
    section = lax.axis_index("section")
    dp = lax.axis_index("dp")
    quarter = dp % 4
    side = dp + 2 * (1 - 2 * ((dp // 2) % 2))
    twin = dp + 1 - 2 * (dp % 2)
    other_quarter = quarter + 2 * (1 - 2 * (quarter // 2))
    barrier = pltpu.get_barrier_semaphore()
    for target in ({"section": 1 - section}, {"dp": side}, {"dp": twin}):
        pl.semaphore_signal(barrier, inc=1, device_id=target, device_id_type=MESH)
    pl.semaphore_wait(barrier, 3)

    gain_out[...] = jnp.zeros_like(gain_out)
    first_gain, second_gain, third_gain = gains[0, 0:1, :], gains[0, 1:2, :], gains[0, 2:3, :]

    def across(src, index):
        return pltpu.make_async_remote_copy(
            src_ref=src, dst_ref=landed.at[index], send_sem=up_send.at[index],
            recv_sem=up_recv.at[index], device_id={"section": 1 - section}, device_id_type=MESH)

    def ctx_part(index):
        return wctx.at[rows_at(index * QUARTER, QUARTER), :]

    def ctx_copy(src, part, target, slot):
        return pltpu.make_async_remote_copy(
            src_ref=src, dst_ref=ctx_part(part), send_sem=ctx_send.at[slot],
            recv_sem=ctx_recv.at[slot], device_id=target, device_id_type=MESH)

    def load(src, dst, slot):
        return pltpu.make_async_copy(src, dst, load_sem.at[slot])

    weight_loads = [
        load(attn_w.at[0, :, 0 : 3 * D], wa.at[:, 0 : 3 * D], 0),
        load(attn_w.at[0, :, 3 * D :], wa.at[:, 3 * D :], 1),
        load(w_in.at[0], wi, 2),
        load(w_out.at[0], wo, 3),
    ]

    def store(src, dst, slot):
        return pltpu.make_async_copy(src, dst, out_sem.at[slot])

    def add_gain(index, row):
        gain_out[index : index + 1, :] = gain_out[index : index + 1, :] + row

    def encoder():
        ctx_copy(
            attn_w.at[0, rows_at(quarter * QUARTER, QUARTER), 4 * D : 6 * D], quarter,
            {"section": 1 - section}, 0,
        ).start()
        rows_in = load(patches, g1.at[0 : patches.shape[0]], 4)
        rows_in.start()
        for copy in weight_loads:
            copy.start()
        rows_in.wait()
        for image in range(MICRO * IMG_MB):
            low_rows = g1[image * PATCHES : (image + 1) * PATCHES, :]
            x[image * IMG_ROWS : image * IMG_ROWS + PATCHES, :] = low_rows
            x[image * IMG_ROWS + PATCHES : (image + 1) * IMG_ROWS, :] = jnp.zeros(
                (IMG_ROWS - PATCHES, D), LOW
            )
        key_bias = jnp.where(
            lax.broadcasted_iota(jnp.int32, (1, IMG_ROWS), 1) < PATCHES, 0.0, MASKED
        )
        key_bias_t = jnp.where(
            lax.broadcasted_iota(jnp.int32, (IMG_ROWS, 1), 0) < PATCHES, 0.0, MASKED
        )

        def forward(micro):
            base = micro * ENC_MB
            rows = rows_at(base, ENC_MB)

            def low_norm(i):
                part = rows_at(base + i * IMG_ROWS, IMG_ROWS)
                a[part, :] = norm_low(x[part, :].astype(WIDE), first_gain)

            loop(IMG_MB, low_norm)

            @pl.when(micro == 0)
            def _():
                weight_loads[0].wait()

            def project(j):
                cols = cols_at(j * D, D)
                qkv[rows, cols] = dot_nn(a[rows, :], wa[:, cols]).astype(LOW)

            loop(3, project)

            def attend(i):
                part = rows_at(base + (i // PAIRS) * IMG_ROWS, IMG_ROWS)
                lane = (i % PAIRS) * PAIR
                o[part, cols_at(lane, PAIR)] = attend_pair(
                    qkv[part, cols_at(lane, PAIR)], qkv[part, cols_at(D + lane, PAIR)],
                    qkv[part, cols_at(2 * D + lane, PAIR)], key_bias,
                )

            loop(IMG_MB * PAIRS, attend)

            @pl.when(micro == 0)
            def _():
                weight_loads[1].wait()

            x1[rows, :] = x[rows, :].astype(WIDE) + dot_nn(o[rows, :], wa[:, 3 * D : 4 * D])

            def mid_norm(i):
                part = rows_at(base + i * IMG_ROWS, IMG_ROWS)
                b[part, :] = norm_low(x1[part, :], second_gain)

            loop(IMG_MB, mid_norm)

            @pl.when(micro == 0)
            def _():
                weight_loads[2].wait()

            def expand(j):
                cols = cols_at(j * 512, 512)
                active, bend = gelu_parts(dot_nn(b[rows, :], wi[:, cols]))
                u[rows, cols] = active.astype(LOW)
                slope[rows, cols] = bend.astype(LOW)

            loop(FF // 512, expand)

            @pl.when(micro == 0)
            def _():
                weight_loads[3].wait()

            x2[rows, :] = x1[rows, :] + dot_nn(u[rows, :], wo[...])

            def top_norm(i):
                part = rows_at(base + i * IMG_ROWS, IMG_ROWS)
                c[part, :] = norm_low(x2[part, :], third_gain)

            loop(IMG_MB, top_norm)
            across(c.at[rows, :], micro).start()

        loop(MICRO, forward)
        stores = [store(a, a_out, 0), store(o, o_out, 1), store(b, b_out, 2), store(u, u_out, 3)]
        for copy in stores:
            copy.start()

        def backward(micro):
            base = micro * ENC_MB
            rows = rows_at(base, ENC_MB)
            across(c.at[rows, :], micro).wait()

            def top_norm(i):
                part = rows_at(base + i * IMG_ROWS, IMG_ROWS)
                upstream = landed[micro, rows_at(i * IMG_ROWS, IMG_ROWS), :].astype(WIDE)
                grad, gain_row = norm_back(upstream, x2[part, :], third_gain)
                x2[part, :] = grad
                g2[part, :] = grad.astype(LOW)
                add_gain(2, gain_row)

            loop(IMG_MB, top_norm)

            def expand(j):
                cols = cols_at(j * D, D)
                hidden = dot_nt(g2[rows, :], wo[cols, :])
                slope[rows, cols] = (hidden * slope[rows, cols].astype(WIDE)).astype(LOW)

            loop(FF // D, expand)
            tmp[0:ENC_MB, :] = dot_nt(slope[rows, :], wi[...])

            def mid_norm(i):
                part = rows_at(base + i * IMG_ROWS, IMG_ROWS)
                grad, gain_row = norm_back(
                    tmp[rows_at(i * IMG_ROWS, IMG_ROWS), :], x1[part, :], second_gain
                )
                grad = grad + x2[part, :]
                x1[part, :] = grad
                g1[part, :] = grad.astype(LOW)
                add_gain(1, gain_row)

            loop(IMG_MB, mid_norm)
            dmix[0:ENC_MB, :] = dot_nt(g1[rows, :], wa[:, 3 * D : 4 * D]).astype(LOW)

            def attend(i):
                part = rows_at(base + (i // PAIRS) * IMG_ROWS, IMG_ROWS)
                lane = (i % PAIRS) * PAIR
                grads = attend_pair_back(
                    qkv[part, cols_at(lane, PAIR)], qkv[part, cols_at(D + lane, PAIR)],
                    qkv[part, cols_at(2 * D + lane, PAIR)],
                    dmix[rows_at((i // PAIRS) * IMG_ROWS, IMG_ROWS), cols_at(lane, PAIR)], key_bias_t,
                )
                for index in range(3):
                    qkv[part, cols_at(index * D + lane, PAIR)] = grads[index]

            loop(IMG_MB * PAIRS, attend)
            tmp[0:ENC_MB, :] = dot_nt(qkv[rows, :], wa[:, 0 : 3 * D])

            def low_norm(i):
                part = rows_at(base + i * IMG_ROWS, IMG_ROWS)
                grad, gain_row = norm_back(
                    tmp[rows_at(i * IMG_ROWS, IMG_ROWS), :], x[part, :].astype(WIDE), first_gain
                )
                x1[part, :] = x1[part, :] + grad
                exch[part, :] = x1[part, HALF:].astype(LOW)
                add_gain(0, gain_row)

            loop(IMG_MB, low_norm)

        loop(MICRO, backward)
        late = [
            store(qkv, dqkv_out, 4), store(g1, g1_out, 5), store(g2, g2_out, 6),
            store(slope, dh_out, 7), store(x1.at[:, 0:HALF], patch_own, 8), store(exch, exch_out, 9),
        ]
        for copy in late:
            copy.start()
        for copy in stores + late:
            copy.wait()
        ctx_copy(
            attn_w.at[0, rows_at(quarter * QUARTER, QUARTER), 4 * D : 6 * D], quarter,
            {"section": 1 - section}, 0,
        ).wait_send()

    def decoder():
        rows_in = load(captions, x.at[0:DEC_ROWS], 4)
        cot_in = load(cot, ct, 5)
        rows_in.start()
        for copy in weight_loads:
            copy.start()
        cot_in.start()
        rows_in.wait()
        full = slice(0, DEC_ROWS)

        def low_norm(i):
            part = rows_at(i * ROW, ROW)
            a[part, :] = norm_low(x[part, :].astype(WIDE), first_gain)

        loop(DEC_ROWS // ROW, low_norm)
        weight_loads[0].wait()

        def project(j):
            cols = cols_at(j * D, D)
            qkv[full, cols] = dot_nn(a[full, :], wa[:, cols]).astype(LOW)

        loop(3, project)

        def segment_pair(row):
            across_rows = jnp.broadcast_to(
                segments[pl.ds(row, 1), :].astype(WIDE), (ROW, ROW)
            )
            return across_rows, across_rows.T

        def self_bias(row, transposed):
            along, down = segment_pair(row)
            sub = lax.broadcasted_iota(jnp.int32, (ROW, ROW), 0)
            lane = lax.broadcasted_iota(jnp.int32, (ROW, ROW), 1)
            order = (lane >= sub) if transposed else (sub >= lane)
            single = jnp.where((along == down) & order, 0.0, MASKED)
            return jnp.concatenate([single, single], 1 if transposed else 0)

        def self_attend(row):
            part = rows_at(row * ROW, ROW)
            row_bias = self_bias(row, False)

            def pair(i):
                lane = i * PAIR
                o[part, cols_at(lane, PAIR)] = attend_pair(
                    qkv[part, cols_at(lane, PAIR)], qkv[part, cols_at(D + lane, PAIR)],
                    qkv[part, cols_at(2 * D + lane, PAIR)], row_bias,
                )

            loop(PAIRS, pair)

        loop(DEC_ROWS // ROW, self_attend)
        weight_loads[1].wait()
        x1[full, :] = x[full, :].astype(WIDE) + dot_nn(o[full, :], wa[:, 3 * D : 4 * D])

        def mid_norm(i):
            part = rows_at(i * ROW, ROW)
            c[part, :] = norm_low(x1[part, :], second_gain)

        loop(DEC_ROWS // ROW, mid_norm)
        cq[...] = dot_nn(c[full, :], wa[:, 4 * D : 5 * D]).astype(LOW)
        weight_loads[3].wait()
        cot_in.wait()

        def cot_project(j):
            cols = cols_at(j * D, D)
            slope[full, cols] = dot_nt(ct[...], wo[cols, :]).astype(LOW)

        loop(FF // D, cot_project)
        weight_loads[2].wait()

        ctx_copy(ctx_part(quarter), quarter, {"section": 1 - section}, 0).wait_recv()
        ctx_copy(ctx_part(quarter), quarter, {"dp": side}, 1).start()
        ctx_copy(ctx_part(quarter), quarter, {"dp": twin}, 2).start()
        ctx_copy(ctx_part(quarter), other_quarter, {"dp": side}, 1).wait_recv()
        ctx_copy(ctx_part(other_quarter), other_quarter, {"dp": twin}, 3).start()
        ctx_copy(ctx_part(quarter), quarter, {"dp": twin}, 2).wait_recv()
        ctx_copy(ctx_part(quarter), quarter, {"dp": twin}, 3).wait_recv()

        def cross_bias(micro):
            key = lax.broadcasted_iota(jnp.int32, (ROW, ENC_MB), 1)
            key_t = lax.broadcasted_iota(jnp.int32, (ENC_MB, ROW), 0)

            def one(i):
                row = micro * ROWS_MB + i
                along, down = segment_pair(row)
                image_along = jnp.zeros((ROW, ROW), WIDE)
                image_down = jnp.zeros((ROW, ROW), WIDE)
                for seg in range(SEGS):
                    image = seg_images[row, seg].astype(WIDE)
                    image_along = jnp.where(along == seg, image, image_along)
                    image_down = jnp.where(down == seg, image, image_down)
                allowed = jnp.zeros((ROW, ENC_MB), jnp.bool_)
                allowed_t = jnp.zeros((ENC_MB, ROW), jnp.bool_)
                for image in range(IMG_MB):
                    low, high = image * IMG_ROWS, image * IMG_ROWS + PATCHES
                    allowed = allowed | (
                        (key >= low) & (key < high) & (image_down[:, 0:1] == image)
                    )
                    allowed_t = allowed_t | (
                        (key_t >= low) & (key_t < high) & (image_along[0:1, :] == image)
                    )
                bias[rows_at(i * ROW, ROW), :] = jnp.where(allowed, 0.0, MASKED)
                bias_t[i] = jnp.where(allowed_t, 0.0, MASKED)

            loop(ROWS_MB, one)

        def cross(micro):
            cross_bias(micro)
            base = micro * DEC_MB
            rows = rows_at(base, DEC_MB)
            keys = rows_at(micro * ENC_MB, ENC_MB)
            across(sent.at[micro], micro).wait_recv()

            def context(j):
                cols = cols_at(j * D, D)
                ctx[keys, cols] = dot_nn(landed[micro], wctx[:, cols]).astype(LOW)

            loop(2, context)

            def attend(i):
                lane = i * PAIR
                half_bias = bias[...]
                co[rows, cols_at(lane, PAIR)] = attend_pair(
                    cq[rows, cols_at(lane, PAIR)], ctx[keys, cols_at(lane, PAIR)],
                    ctx[keys, cols_at(D + lane, PAIR)], jnp.concatenate([half_bias, half_bias], 0),
                )

            loop(PAIRS, attend)
            x2[rows, :] = x1[rows, :] + dot_nn(co[rows, :], wa[:, 5 * D : 6 * D])

            def top_norm(i):
                part = rows_at(base + i * ROW, ROW)
                b[part, :] = norm_low(x2[part, :], third_gain)

            loop(ROWS_MB, top_norm)

            def expand(j):
                cols = cols_at(j * 512, 512)
                active, bend = gelu_parts(dot_nn(b[rows, :], wi[:, cols]))
                u[rows, cols] = active.astype(LOW)
                slope[rows, cols] = (bend * slope[rows, cols].astype(WIDE)).astype(LOW)

            loop(FF // 512, expand)
            tmp[0:DEC_MB, :] = dot_nt(slope[rows, :], wi[...])

            def top_back(i):
                part = rows_at(base + i * ROW, ROW)
                grad, gain_row = norm_back(tmp[rows_at(i * ROW, ROW), :], x2[part, :], third_gain)
                grad = grad + ct[part, :].astype(WIDE)
                g2w[part, :] = grad
                g2[part, :] = grad.astype(LOW)
                add_gain(2, gain_row)

            loop(ROWS_MB, top_back)
            dmix[0:DEC_MB, :] = dot_nt(g2[rows, :], wa[:, 5 * D : 6 * D]).astype(LOW)

            def attend_back(i):
                lane = i * PAIR
                parts = [bias_t[j] for j in range(ROWS_MB)]
                grads = attend_pair_back(
                    cq[rows, cols_at(lane, PAIR)], ctx[keys, cols_at(lane, PAIR)],
                    ctx[keys, cols_at(D + lane, PAIR)], dmix[0:DEC_MB, cols_at(lane, PAIR)],
                    jnp.concatenate(parts + parts, 1),
                )
                cq[rows, cols_at(lane, PAIR)] = grads[0]
                ctx[keys, cols_at(lane, PAIR)] = grads[1]
                ctx[keys, cols_at(D + lane, PAIR)] = grads[2]

            loop(PAIRS, attend_back)
            sent[micro] = dot_nt(ctx[keys, :], wctx[...]).astype(LOW)
            across(sent.at[micro], micro).start()

        loop(MICRO, cross)
        stores = [
            store(a.at[full], a_out.at[full], 0), store(o.at[full], o_out.at[full], 1),
            store(b.at[full], b_out.at[full], 2), store(u.at[full], u_out.at[full], 3),
            store(slope.at[full], dh_out.at[full], 7), store(g2.at[full], g2_out.at[full], 6),
            store(co, co_out, 10), store(cq, dq_out, 11), store(landed, up_out, 12),
            store(ctx, dctx_out, 13), store(c.at[full], c_out.at[full], 14),
        ]
        for copy in stores:
            copy.start()

        def finish(micro):
            base = micro * DEC_MB
            rows = rows_at(base, DEC_MB)
            tmp[0:DEC_MB, :] = dot_nt(cq[rows, :], wa[:, 4 * D : 5 * D])

            def mid_back(i):
                part = rows_at(base + i * ROW, ROW)
                grad, gain_row = norm_back(tmp[rows_at(i * ROW, ROW), :], x1[part, :], second_gain)
                grad = grad + g2w[part, :]
                x1[part, :] = grad
                g1[part, :] = grad.astype(LOW)
                add_gain(1, gain_row)

            loop(ROWS_MB, mid_back)
            dmix[0:DEC_MB, :] = dot_nt(g1[rows, :], wa[:, 3 * D : 4 * D]).astype(LOW)

            def self_back(i):
                part = rows_at(base + i * ROW, ROW)
                row_bias = self_bias(micro * ROWS_MB + i, True)

                def pair(j):
                    lane = j * PAIR
                    grads = attend_pair_back(
                        qkv[part, cols_at(lane, PAIR)], qkv[part, cols_at(D + lane, PAIR)],
                        qkv[part, cols_at(2 * D + lane, PAIR)],
                        dmix[rows_at(i * ROW, ROW), cols_at(lane, PAIR)], row_bias,
                    )
                    for index in range(3):
                        qkv[part, cols_at(index * D + lane, PAIR)] = grads[index]

                loop(PAIRS, pair)

            loop(ROWS_MB, self_back)
            tmp[0:DEC_MB, :] = dot_nt(qkv[rows, :], wa[:, 0 : 3 * D])

            def low_back(i):
                part = rows_at(base + i * ROW, ROW)
                grad, gain_row = norm_back(
                    tmp[rows_at(i * ROW, ROW), :], x[part, :].astype(WIDE), first_gain
                )
                x1[part, :] = x1[part, :] + grad
                exch[rows_at(DEC_ROWS + base + i * ROW, ROW), :] = x1[part, 0:HALF].astype(LOW)
                add_gain(0, gain_row)

            loop(ROWS_MB, low_back)
            decoded = (x2[rows, :] + dot_nn(u[rows, :], wo[...])).astype(LOW)
            exch[rows, :] = decoded[:, 0:HALF]
            decoded_half[rows, :] = decoded[:, HALF:]

        loop(MICRO, finish)
        late = [
            store(qkv.at[full], dqkv_out.at[full], 4), store(g1.at[full], g1_out.at[full], 5),
            store(x1.at[full, HALF:], caption_own, 8), store(exch, exch_out, 9),
            store(decoded_half, decoded_own, 15),
        ]
        for copy in late:
            copy.start()
        for copy in stores + late:
            copy.wait()
        for micro in range(MICRO):
            across(sent.at[micro], micro).wait_send()
        ctx_copy(ctx_part(quarter), quarter, {"dp": side}, 1).wait_send()
        ctx_copy(ctx_part(quarter), quarter, {"dp": twin}, 2).wait_send()
        ctx_copy(ctx_part(quarter), quarter, {"dp": twin}, 3).wait_send()

    @pl.when(section == 0)
    def _():
        encoder()

    @pl.when(section == 1)
    def _():
        decoder()


def main_call(patches, captions, segments, seg_images, attn_w, w_in, w_out, gains, cot):
    def low(*shape):
        return jax.ShapeDtypeStruct(shape, LOW)

    def wide(*shape):
        return jax.ShapeDtypeStruct(shape, WIDE)

    outs = [
        low(ENC_ROWS, D), low(ENC_ROWS, D), low(DEC_ROWS, D), low(ENC_ROWS, D), low(ENC_ROWS, FF),
        low(ENC_ROWS, 3 * D), low(ENC_ROWS, D), low(ENC_ROWS, D), low(ENC_ROWS, FF),
        low(DEC_ROWS, D), low(DEC_ROWS, D), low(MICRO, ENC_MB, D), low(ENC_ROWS, 2 * D),
        wide(8, D), wide(ENC_ROWS, HALF), low(DEC_ROWS, HALF), wide(DEC_ROWS, HALF),
        low(2 * DEC_ROWS, HALF),
    ]
    any_spec = pl.BlockSpec(memory_space=pl.ANY)
    vmem_spec = pl.BlockSpec(memory_space=pltpu.VMEM)
    out_specs = [any_spec] * len(outs)
    out_specs[13] = vmem_spec
    vmem = pltpu.VMEM
    scratch = [
        vmem((D, 6 * D), LOW), vmem((D, FF), LOW), vmem((FF, D), LOW), vmem((D, 2 * D), LOW),
        vmem((ENC_ROWS, D), LOW), vmem((DEC_ROWS, D), LOW),
        vmem((ENC_ROWS, D), LOW), vmem((ENC_ROWS, D), LOW), vmem((ENC_ROWS, D), LOW),
        vmem((ENC_ROWS, D), LOW),
        vmem((ENC_ROWS, 3 * D), LOW), vmem((ENC_ROWS, FF), LOW), vmem((ENC_ROWS, FF), LOW),
        vmem((ENC_ROWS, D), WIDE), vmem((ENC_ROWS, D), WIDE),
        vmem((ENC_ROWS, D), LOW), vmem((ENC_ROWS, D), LOW),
        vmem((MICRO, ENC_MB, D), LOW), vmem((max(ENC_MB, DEC_ROWS), D), LOW),
        vmem((ENC_ROWS, 2 * D), LOW),
        vmem((DEC_ROWS, D), LOW), vmem((DEC_ROWS, D), LOW), vmem((DEC_ROWS, D), WIDE),
        vmem((ENC_MB, D), WIDE), vmem((MICRO, ENC_MB, D), LOW),
        vmem((DEC_MB, ENC_MB), WIDE), vmem((ROWS_MB, ENC_MB, ROW), WIDE),
        vmem((2 * DEC_ROWS, HALF), LOW), vmem((DEC_ROWS, HALF), LOW),
        pltpu.SemaphoreType.DMA((6,)), pltpu.SemaphoreType.DMA((16,)),
        pltpu.SemaphoreType.DMA((MICRO,)), pltpu.SemaphoreType.DMA((MICRO,)),
        pltpu.SemaphoreType.DMA((4,)), pltpu.SemaphoreType.DMA((4,)),
    ]
    return pl.pallas_call(
        main_kernel,
        name="layers",
        out_shape=outs,
        in_specs=[any_spec, any_spec, vmem_spec, pl.BlockSpec(memory_space=pltpu.SMEM)]
        + [any_spec] * 3 + [vmem_spec, any_spec],
        out_specs=out_specs,
        scratch_shapes=scratch,
        compiler_params=pltpu.CompilerParams(
            collective_id=1, has_side_effects=True, vmem_limit_bytes=63 * MIB
        ),
    )(patches, captions, segments, seg_images, attn_w, w_in, w_out, gains, cot)


CHUNK = 256
SLOTS = 8
FIRST_LAG = 2
LAG = 2
GAIN_STEPS = 5
OUT_IDS = 12
ONLY_DEC = 12
CTX_IDS = 6


def grads_kernel(n_bits, *refs):
    (
        a_in, o_in, c_in, b_in, u_in, dqkv_in, g1_in, g2_in, dh_in, co_in, dq_in, up_in, dctx_in,
        gains_in, patch_own, decoded_own, caption_own, exch_in, cot_in,
        shares, gains_out, patch_out, decoded_out, caption_out,
        a, o, c, b, u, dqkv, g1, g2, dh, co, dq, up, dctx, cot,
        part, ctx_sum, exch, patch_rows, gain_sum, gain_in,
    ) = refs[:44]
    recv = refs[44 : 44 + n_bits]
    load_sem, own_sem, send_sem, recv_sem, gain_send, gain_recv, far_send, far_recv = refs[44 + n_bits :]
    section = lax.axis_index("section")
    dp = lax.axis_index("dp")
    bits = [(dp // (1 << k)) % 2 for k in range(n_bits)]
    partners = [{"dp": dp + (1 << k) * (1 - 2 * bits[k])} for k in range(n_bits)]
    across = {"section": 1 - section}
    barrier = pltpu.get_barrier_semaphore()
    for target in partners + [across]:
        pl.semaphore_signal(barrier, inc=1, device_id=target, device_id_type=MESH)
    pl.semaphore_wait(barrier, n_bits + 1)

    rows = part.shape[-2]
    owners = 1 << n_bits
    total = recv[0].shape[0]
    begin = ONLY_DEC * (1 - section)

    def remote(src, dst, send, receive, target):
        return pltpu.make_async_remote_copy(
            src_ref=src, dst_ref=dst, send_sem=send, recv_sem=receive, device_id=target,
            device_id_type=MESH)

    def gain_copy(k):
        return remote(gain_sum.at[k], gain_in.at[k], gain_send.at[k], gain_recv.at[k], partners[k])

    def exch_copy():
        return remote(exch_in, exch, far_send.at[0], far_recv.at[0], across)

    def ctx_copy():
        return remote(ctx_sum, shares.at[0:CTX_IDS], far_send.at[1], far_recv.at[1], across)

    gain_sum[0] = gains_in[...]
    gain_copy(0).start()

    def load_plan(is_dec):
        count = DEC_ROWS if is_dec else ENC_ROWS

        def short(src, dst):
            return src.at[0:count], dst.at[0:count]

        plan = {
            0: short(u_in, u), 1: short(g2_in, g2), 2: short(b_in, b), 3: short(dh_in, dh),
            4: short(a_in, a), 5: short(dqkv_in, dqkv), 6: short(o_in, o), 7: short(g1_in, g1),
        }
        if is_dec:
            only = {
                8: (up_in, up), 9: (dctx_in, dctx), 10: (c_in, c), 11: (dq_in, dq),
                12: (co_in, co), 13: (cot_in, cot),
            }
            plan = {**only, **plan}
        return plan

    def need(is_dec, *slots):
        plan = load_plan(is_dec)
        for slot in slots:
            pltpu.make_async_copy(*plan[slot], load_sem.at[slot]).wait()

    for is_dec in (False, True):
        @pl.when(section == int(is_dec))
        def _(is_dec=is_dec):
            for slot, (src, dst) in load_plan(is_dec).items():
                pltpu.make_async_copy(src, dst, load_sem.at[slot]).start()
            if is_dec:
                pltpu.make_async_copy(decoded_own, decoded_out, load_sem.at[14]).start()
                pltpu.make_async_copy(caption_own, caption_out, load_sem.at[15]).start()
            else:
                pltpu.make_async_copy(patch_own, patch_rows, load_sem.at[14]).start()

    def core_copy(index):
        slot = index % SLOTS
        return remote(part.at[slot, 1 - bits[0]], recv[0].at[index], send_sem.at[0, index],
                      recv_sem.at[0, index], partners[0])

    def stage_copy(stage, index):
        keep = (slice(None),) * (n_bits - 1 - stage)
        return remote(
            recv[stage - 1].at[(index,) + keep + (1 - bits[stage],)], recv[stage].at[index],
            send_sem.at[stage, index], recv_sem.at[stage, index], partners[stage])

    def advance(i):
        for stage in range(n_bits):
            j = i - FIRST_LAG - stage * LAG

            @pl.when((j >= begin) & (j < total))
            def _(stage=stage, j=j):
                if stage == 0:
                    core_copy(j).wait()
                    mine = part[j % SLOTS, bits[0]]
                else:
                    stage_copy(stage, j).wait()
                    keep = (slice(None),) * (n_bits - 1 - stage)
                    mine = recv[stage - 1][(j,) + keep + (bits[stage],)]
                summed = mine.astype(WIDE) + recv[stage][j].astype(WIDE)
                if stage < n_bits - 1:
                    recv[stage][j] = summed.astype(LOW)
                    stage_copy(stage + 1, j).start()
                else:
                    @pl.when(j < CTX_IDS)
                    def _():
                        ctx_sum[j] = summed

                    @pl.when(j >= CTX_IDS)
                    def _():
                        shares[j - CTX_IDS] = summed

                    @pl.when(j == CTX_IDS - 1)
                    def _():
                        ctx_copy().start()
        for k in range(n_bits):
            @pl.when(i == ONLY_DEC + GAIN_STEPS * (k + 1))
            def _(k=k):
                gain_copy(k).wait()
                summed = gain_sum[k] + gain_in[k]
                if k == n_bits - 1:
                    gains_out[...] = summed
                else:
                    gain_sum[k + 1] = summed
                    gain_copy(k + 1).start()

    def place(index, first_owner, block):
        for k in range(block.shape[0] // rows):
            owner = first_owner + k
            path = tuple((owner >> bit) & 1 for bit in reversed(range(1, n_bits)))
            part[(index % SLOTS, owner & 1) + path] = block[k * rows : (k + 1) * rows].astype(LOW)

    def simple_phase(first, count, left, right, col, row_count):
        def step(i):
            index = first + i
            cols = cols_at(col + i * CHUNK, CHUNK)
            if row_count is None:
                value = dot_tn(left[...].reshape(-1, D), right[:, cols])
            else:
                value = dot_tn(left[0:row_count, :], right[0:row_count, cols])
            place(index, 0, value)
            core_copy(index).start()
            advance(index)
        loop(count, step)

    def out_phase(first, right, row_count):
        share = FF // owners
        blocks = share // rows
        step_owners = D // share

        def step(i):
            cols = cols_at(i * CHUNK, CHUNK)
            base = first + i * blocks
            for piece in range(FF // D):
                value = dot_tn(u[0:row_count, piece * D : (piece + 1) * D], right[0:row_count, cols])
                for k in range(step_owners):
                    for q in range(blocks):
                        low = k * share + q * rows
                        place(base + q, piece * step_owners + k, value[low : low + rows])
            loop(blocks, lambda q: core_copy(base + q).start())
            loop(blocks, lambda q: advance(base + q))
        loop(D // CHUNK, step)

    @pl.when(section == 1)
    def _():
        need(True, 8, 9)
        simple_phase(0, CTX_IDS, up, dctx, 0, None)
        need(True, 10, 11)
        simple_phase(CTX_IDS, 3, c, dq, 0, DEC_ROWS)
        need(True, 12, 1)
        simple_phase(CTX_IDS + 3, 3, co, g2, 0, DEC_ROWS)

    for is_dec in (False, True):
        @pl.when(section == int(is_dec))
        def _(is_dec=is_dec):
            count = DEC_ROWS if is_dec else ENC_ROWS
            need(is_dec, 0, 13 if is_dec else 1)
            out_phase(ONLY_DEC, cot if is_dec else g2, count)
            need(is_dec, 2, 3)
            simple_phase(ONLY_DEC + OUT_IDS, FF // CHUNK, b, dh, 0, count)

    exch_copy().start()

    for is_dec in (False, True):
        @pl.when(section == int(is_dec))
        def _(is_dec=is_dec):
            count = DEC_ROWS if is_dec else ENC_ROWS
            need(is_dec, 4, 5)
            first = ONLY_DEC + OUT_IDS + FF // CHUNK
            simple_phase(first, 3 * D // CHUNK, a, dqkv, 0, count)
            need(is_dec, 6, 7)
            simple_phase(first + 3 * D // CHUNK, D // CHUNK, o, g1, 0, count)

    exch_copy().wait()

    @pl.when(section == 0)
    def _():
        pltpu.make_async_copy(patch_own, patch_rows, load_sem.at[14]).wait()
        for image in range(MICRO * IMG_MB):
            patch_out[image * PATCHES : (image + 1) * PATCHES, :] = patch_rows[
                image * IMG_ROWS : image * IMG_ROWS + PATCHES, :
            ]
        decoded_out[...] = exch[0:DEC_ROWS, :]
        caption_out[...] = exch[DEC_ROWS : 2 * DEC_ROWS, :].astype(WIDE)

    @pl.when(section == 1)
    def _():
        pltpu.make_async_copy(decoded_own, decoded_out, load_sem.at[14]).wait()
        pltpu.make_async_copy(caption_own, caption_out, load_sem.at[15]).wait()
        for image in range(MICRO * IMG_MB):
            patch_out[image * PATCHES : (image + 1) * PATCHES, :] = exch[
                image * IMG_ROWS : image * IMG_ROWS + PATCHES, :
            ].astype(WIDE)

    loop(FIRST_LAG + (n_bits - 1) * LAG, lambda i: advance(total + i))

    @pl.when(section == 0)
    def _():
        ctx_copy().wait_recv()

    @pl.when(section == 1)
    def _():
        ctx_copy().wait_send()


def grads_call(n_dp, *operands):
    n_bits = n_dp.bit_length() - 1
    rows = D // n_dp
    share = FF // n_dp
    total = ONLY_DEC + 2 * OUT_IDS + 4 * D // CHUNK
    vmem = pltpu.VMEM
    pair = (2,) * (n_bits - 1)
    any_spec = pl.BlockSpec(memory_space=pl.ANY)
    vmem_spec = pl.BlockSpec(memory_space=pltpu.VMEM)
    sem = pltpu.SemaphoreType.DMA
    scratch = [
        vmem((ENC_ROWS, D), LOW), vmem((ENC_ROWS, D), LOW), vmem((DEC_ROWS, D), LOW),
        vmem((ENC_ROWS, D), LOW), vmem((ENC_ROWS, FF), LOW), vmem((ENC_ROWS, 3 * D), LOW),
        vmem((ENC_ROWS, D), LOW), vmem((ENC_ROWS, D), LOW), vmem((ENC_ROWS, FF), LOW),
        vmem((DEC_ROWS, D), LOW), vmem((DEC_ROWS, D), LOW), vmem((MICRO, ENC_MB, D), LOW),
        vmem((ENC_ROWS, 2 * D), LOW), vmem((DEC_ROWS, D), LOW),
        vmem((SLOTS, 2) + pair + (rows, CHUNK), LOW), vmem((CTX_IDS, rows, CHUNK), WIDE),
        vmem((2 * DEC_ROWS, HALF), LOW), vmem((ENC_ROWS, HALF), WIDE),
        vmem((n_bits, 8, D), WIDE), vmem((n_bits, 8, D), WIDE),
    ]
    scratch += [vmem((total,) + pair[k:] + (rows, CHUNK), LOW) for k in range(n_bits)]
    scratch += [
        sem((16,)), sem((1,)), sem((n_bits, total)), sem((n_bits, total)), sem((n_bits,)),
        sem((n_bits,)), sem((2,)), sem((2,)),
    ]
    in_specs = [any_spec] * len(operands)
    in_specs[13] = vmem_spec
    return pl.pallas_call(
        functools.partial(grads_kernel, n_bits),
        name="weight_sums",
        out_shape=(
            jax.ShapeDtypeStruct((total - CTX_IDS, rows, CHUNK), WIDE),
            jax.ShapeDtypeStruct((8, D), WIDE),
            jax.ShapeDtypeStruct((MICRO * IMG_MB * PATCHES, HALF), WIDE),
            jax.ShapeDtypeStruct((DEC_ROWS, HALF), LOW),
            jax.ShapeDtypeStruct((DEC_ROWS, HALF), WIDE),
        ),
        in_specs=in_specs,
        out_specs=(vmem_spec,) * 5,
        scratch_shapes=scratch,
        compiler_params=pltpu.CompilerParams(
            collective_id=2, has_side_effects=True, vmem_limit_bytes=63 * MIB
        ),
    )(*operands)


def pick_columns(chunks, rows, columns):
    shaped = chunks.reshape(columns // CHUNK, rows // chunks.shape[1], chunks.shape[1], CHUNK)
    return shaped.transpose(1, 2, 0, 3).reshape(rows, columns)


def kernel_sums(n_dp, operands):
    chunks, gain_sums, patch_out, decoded_out, caption_out = grads_call(n_dp, *operands)
    rows = D // n_dp
    last = CTX_IDS
    outer = last + OUT_IDS
    inner = outer + OUT_IDS
    attn_share = jnp.concatenate(
        [pick_columns(chunks[inner:], rows, 4 * D), pick_columns(chunks[:last], rows, 2 * D)], 1
    )
    in_share = pick_columns(chunks[outer:inner], rows, FF)
    out_share = pick_columns(chunks[last:outer], FF // n_dp, D)
    own_gains = lax.dynamic_slice_in_dim(gain_sums[:3], lax.axis_index("dp") * rows, rows, 1)
    return decoded_out, caption_out, patch_out, attn_share, in_share, out_share, own_gains


def shifted(block, distance):
    devices = range(lax.axis_size("section"))
    route = [(i - distance, i) for i in devices if i - distance in devices]
    return lax.ppermute(block, "section", route)


def plain_sums(operands):
    (
        a, o, c, b, u, dqkv, g1, g2, dh, co, dq, up, dctx,
        gains, patch_own, decoded_own, caption_own, exch, cot,
    ) = operands
    is_first = lax.axis_index("section") == 0
    up = up.reshape(ENC_ROWS, D)

    def encoder_parts():
        return (
            jnp.concatenate([dot_tn(a, dqkv), dot_tn(o, g1)], 1), jnp.zeros((D, 2 * D), WIDE),
            jnp.zeros((D, 2 * D), WIDE), dot_tn(b, dh), dot_tn(u, g2),
        )

    def decoder_parts():
        rows = slice(0, DEC_ROWS)
        return (
            jnp.concatenate([dot_tn(a[rows], dqkv[rows]), dot_tn(o[rows], g1[rows])], 1),
            jnp.concatenate([dot_tn(c, dq), dot_tn(co, g2[rows])], 1),
            dot_tn(up, dctx), dot_tn(b[rows], dh[rows]), dot_tn(u[rows], cot),
        )

    parts = lax.cond(is_first, encoder_parts, decoder_parts)
    sums = [lax.psum_scatter(part, "dp", scatter_dimension=0, tiled=True) for part in parts]
    last = jnp.where(is_first, shifted(sums[2], -1), sums[1])
    moved = lax.ppermute(exch, "section", [(0, 1), (1, 0)])

    def unpad(block):
        shaped = block[:ENC_ROWS].reshape(MICRO * IMG_MB, IMG_ROWS, HALF)
        return shaped[:, :PATCHES].reshape(-1, HALF).astype(WIDE)

    return (
        jnp.where(is_first, moved[:DEC_ROWS], decoded_own),
        jnp.where(is_first, moved[DEC_ROWS:].astype(WIDE), caption_own),
        jnp.where(is_first, unpad(patch_own), unpad(moved)),
        jnp.concatenate([sums[0], last], 1),
        sums[3],
        sums[4],
        lax.psum_scatter(gains[:3], "dp", scatter_dimension=1, tiled=True),
    )


def local(patches, captions, segments, seg_images, attn_w, w_in, w_out, norm_gains, cotangent):
    n_dp = lax.axis_size("dp")
    kept = main_call(
        patches, captions, segments, seg_images, attn_w, w_in, w_out, norm_gains, cotangent
    )
    operands = list(kept) + [cotangent]
    if n_dp & (n_dp - 1) == 0 and (D // n_dp) % 16 == 0:
        results = kernel_sums(n_dp, operands)
    else:
        results = plain_sums(operands)
    return results[:3] + tuple(share[None] for share in results[3:])


def solution(mesh):
    placed = (
        P("dp", None),
        P("dp", None),
        P("dp", None),
        P("dp", None),
        P("section", None, None),
        P("section", None, None),
        P("section", None, None),
        P("section", None, None),
        P("dp", None),
    )
    return jax.shard_map(
        local,
        mesh=mesh,
        in_specs=placed,
        out_specs=(
            P("dp", "section"),
            P("dp", "section"),
            P("dp", "section"),
            P("section", "dp", None),
            P("section", "dp", None),
            P("section", "dp", None),
            P("section", None, "dp"),
        ),
        check_vma=False,
    )
```

time: 1070 us -> 262 us (0.24)
  the two profiles are of different devices: /device:TPU:0 before, /device:TPU:6 now
where the time goes in v2:
time: 262 us
  Pallas kernels  250 us (95%)
  local copies, waits for them, and re-layouts  9.69 us (4%)
    pallas_call x1, Pallas kernels, grads_call(): pl.pallas_call(functools.partial(grads_kernel, n_bits), name='weight_sums...  140 us
    pallas_call x1, Pallas kernels, main_call(): pl.pallas_call(main_kernel, name='layers', out_shape=outs, in_specs=[any_...  110 us

profile of v2, /device:TPU:6, one launch (start us, length us, event | category | flops | bytes accessed | tf_op | source)
XLA Modules:
  0.0 261.7 jit_solution(3782775688530580376)
XLA Ops:
  0.6 1.3 copy.18.refs_7_
  1.9 109.9 %layers.1 = (bf16[832,768]{1,0:T(8,128)(2,1)}, bf16[832,768]{1,0:T(8,128)(2,1)}, bf16[512,768]{1,0:T(8,128)(2,1)}, bf16[832,768]{1,0:T(8,128)(2,1)}, bf16[832,30...) custom-call(bf16[784,768]{1,0:T(8,128)(2,1)} %refs_0_.1, ...), custom_call_target="tpu_custom_call" | custom-call | tf_op jit(solution)/shard_map/layers/pallas_call | solution.py:644
  111.9 140.4 %weight_sums.1 = (f32[42,48,256]{2,1,0:T(8,128)}, f32[8,768]{1,0:T(8,128)}, f32[784,384]{1,0:T(8,128)}, bf16[512,384]{1,0:T(8,128)(2,1)}, f32[512,384]{1,0:T(8,128)}) custom-call(bf16[832,768]{1,0:T(8,128)(2,1)} %get-tuple-element.30.refs_0_, bf16[832,768]{1,0:T(8,128)(2,1)} %get-tuple-element.31.refs_1_, bf16[512,768]{1,0:T(8,128)(2,1)} %get-tuple-element.32.refs_2_, ...), custom_call_target="tpu_custom_call" | custom-call | tf_op jit(solution)/shard_map/weight_sums/pallas_call | solution.py:921
  252.3 1.5 fusion
  253.9 1.0 fusion.1
  254.9 1.0 maximum_bitcast_fusion
  255.9 0.0 copy-start.3
  255.9 0.0 copy-start.2
  255.9 0.0 copy-start.1
  255.9 0.4 copy.29
  256.3 1.2 broadcast_in_dim_reshape.7
  257.5 0.0 copy-start
  257.5 0.9 copy.23
  258.4 0.0 copy-done.3
  258.4 0.1 constant_dynamic-slice_fusion
  258.5 0.6 broadcast_in_dim.7
  259.0 0.0 copy-done.2
  259.0 0.7 copy.33
  259.8 0.0 copy-done.1
  259.8 0.9 copy.34
  260.7 0.0 copy-done
  260.7 1.0 copy.35
  (3 shorter events, 0.1 us)
Async XLA Ops:
  255.9 2.5 copy-start.3
  255.9 3.2 %copy-start.2 = (bf16[512,384]{1,0:T(8,128)(2,1)S(1)}, bf16[512,384]{1,0:T(8,128)(2,1)}, u32[]{:S(2)}) copy-start(bf16[512,384]{1,0:T(8,128)(2,1)} %get-tuple-element.63) | copy-start | bytes 1179652
  255.9 3.9 %copy-start.1 = (f32[512,384]{1,0:T(8,128)S(1)}, f32[512,384]{1,0:T(8,128)}, u32[]{:S(2)}) copy-start(f32[512,384]{1,0:T(8,128)} %get-tuple-element.64) | copy-start | bytes 2359300
  257.5 3.2 %copy-start = (f32[784,384]{1,0:T(8,128)S(1)}, f32[784,384]{1,0:T(8,128)}, u32[]{:S(2)}) copy-start(f32[784,384]{1,0:T(8,128)} %get-tuple-element.65) | copy-start | bytes 3612676
